TPU v7x, 32 devices: a whole 2x2x4 slice. The times are simulated.
32 devices in a mesh: dp: 8 (over y, x, core), blk: 4 (over z).
Axes of the slice: x: 2, y: 2, z: 4, core: 2. Of those that a mesh axis runs over, the one named last changes fastest.
Arguments:
- tokens: bfloat16 [32, 512, 768], P('dp', 'blk'), may hold values from -6 to 6
- row_kinds: int32 [32], P('dp'), may hold values from 0 to 1, as said below
- live_mask: int32 [32, 512], P('dp', 'blk'), may hold values from 0 to 1, as said below
- keep_flag: int32 [32], P('dp'), may hold values 0 or 1
- projection: bfloat16 [768, 2304], replicated, may hold values from -0.21875 to 0.21875
- proj_bias: bfloat16 [2, 768], replicated, may hold values from -3 to 3
- mixing: bfloat16 [768, 768], replicated, may hold values from -3.5 to 3.5
- mix_bias: bfloat16 [768], replicated, may hold values from -2 to 2
- attn_gain: bfloat16 [768], replicated, may hold values from 0.5 to 1.5
- attn_shift: bfloat16 [768], replicated, may hold values from -2 to 2
- expand: bfloat16 [768, 3072], replicated, may hold values from -0.21875 to 0.21875
- expand_bias: bfloat16 [3072], replicated, may hold values from -3 to 3
- contract: bfloat16 [3072, 768], replicated, may hold values from -0.109375 to 0.109375
- contract_bias: bfloat16 [768], replicated, may hold values from -2 to 2
- ffn_gain: bfloat16 [768], replicated, may hold values from 0.5 to 1.5
- ffn_shift: bfloat16 [768], replicated, may hold values from -2 to 2
- cotangent: bfloat16 [32, 512, 768], P('dp', 'blk'), may hold values from -6 to 6
Outputs:
- layer_out: bfloat16 [32, 512, 768], P('dp', 'blk')
- tokens_grad: float32 [32, 512, 768], P('dp', 'blk')
- projection_grad: float32 [768, 2304], replicated
- proj_bias_grad: float32 [2, 768], replicated
- mixing_grad: float32 [768, 768], replicated
- mix_bias_grad: float32 [768], replicated
- attn_gain_grad: float32 [768], replicated
- attn_shift_grad: float32 [768], replicated
- expand_grad: float32 [768, 3072], replicated
- expand_bias_grad: float32 [3072], replicated
- contract_grad: float32 [3072, 768], replicated
- contract_bias_grad: float32 [768], replicated
- ffn_gain_grad: float32 [768], replicated
- ffn_shift_grad: float32 [768], replicated
Inputs may be any that keep to these rules, and one draw needn't show every extreme that they name: `row_kinds`: in each aligned group of 4 rows at least one row has kind 1. `live_mask`: each row is live on a prefix of its positions; fewer than 128 last positions of a row are padding.
All inputs are finite; a program needn't handle non-finite values. No bound on the sum of `keep_flag` on one device may be relied on, other than what follows from the above.
Results may differ from a plain program's by a relative error of at most 0.014.
Values may be sent and summed in bfloat16 or wider, within the bound.
A program may use at most 192 MiB of HBM per device.

v0:
```python
from functools import partial

import jax
import jax.numpy as jnp
from jax import lax
from jax.sharding import PartitionSpec as P

D = 768
HEADS = 12
HEAD_DIM = 64
DOC_SHORT = 128


norm_eps = 1e-05
masked_value = -1000000000.0


def layer_norm(hidden, gain_vec, shift_vec):
    row_mean = jnp.mean(hidden, axis=-1, keepdims=True)
    centered = hidden - row_mean
    variance = jnp.mean(centered * centered, axis=-1, keepdims=True)
    return centered * lax.rsqrt(variance + norm_eps) * gain_vec + shift_vec


def split_heads(matrix):
    return matrix.reshape(matrix.shape[0], HEADS, HEAD_DIM)


def masked_scores(query_side, key_side, query_seg, key_seg, key_live):
    scores = jnp.einsum(
        "qhd,khd->hqk",
        split_heads(query_side),
        split_heads(key_side),
        preferred_element_type=jnp.float32,
    ) * HEAD_DIM ** (-0.5)
    allowed = (query_seg[:, None] == key_seg[None, :]) & (key_live[None, :] > 0)
    return jnp.where(allowed[None], scores, masked_value)


def attend_row(bundle):
    queries_row, keys_row, values_row, query_seg, key_seg, key_live = bundle
    scores = masked_scores(queries_row, keys_row, query_seg, key_seg, key_live)
    row_max = jnp.max(scores, axis=-1, keepdims=True)
    shifted = jnp.exp(scores - row_max)
    row_total = jnp.sum(shifted, axis=-1, keepdims=True)
    soft_probs = shifted / row_total
    log_total = row_max + jnp.log(row_total)
    attended = jnp.einsum(
        "hqk,khd->qhd",
        soft_probs.astype(jnp.bfloat16),
        split_heads(values_row),
        preferred_element_type=jnp.float32,
    )
    return (attended.reshape(-1, D).astype(jnp.bfloat16), log_total[..., 0])


def query_grad_row(with_keys, bundle):
    queries_row, keys_row, values_row, query_seg, key_seg, key_live, log_total, dmix_row = bundle
    scores = masked_scores(queries_row, keys_row, query_seg, key_seg, key_live)
    soft_probs = jnp.exp(scores - log_total[..., None])
    dmix_heads = split_heads(dmix_row)
    d_prob = jnp.einsum(
        "qhd,khd->hqk", dmix_heads, split_heads(values_row), preferred_element_type=jnp.float32
    )
    delta = jnp.sum(soft_probs * d_prob, axis=-1)
    d_score = (soft_probs * (d_prob - delta[..., None])).astype(jnp.bfloat16)
    d_queries = jnp.einsum(
        "hqk,khd->qhd", d_score, split_heads(keys_row), preferred_element_type=jnp.float32
    )
    d_queries = (d_queries * HEAD_DIM ** (-0.5)).reshape(-1, D).astype(jnp.bfloat16)
    d_keys = jnp.einsum(
        "hqk,qhd->khd", d_score, split_heads(queries_row), preferred_element_type=jnp.float32
    )
    d_keys = (d_keys * HEAD_DIM ** (-0.5)).reshape(-1, D)
    d_values = jnp.einsum(
        "hqk,qhd->khd",
        soft_probs.astype(jnp.bfloat16),
        dmix_heads,
        preferred_element_type=jnp.float32,
    ).reshape(-1, D)
    return (d_queries, delta, d_keys, d_values)


def local(
    tokens,
    row_kinds,
    live_mask,
    keep_flag,
    projection,
    proj_bias,
    mixing,
    mix_bias,
    attn_gain,
    attn_shift,
    expand,
    expand_bias,
    contract,
    contract_bias,
    ffn_gain,
    ffn_shift,
    cotangent,
):
    row_count, block_len, model_width = tokens.shape
    cycle_size = lax.axis_size("blk")
    length = block_len * cycle_size
    flat_tokens = tokens.reshape(row_count * block_len, model_width)
    token_values = flat_tokens.astype(jnp.float32)
    projected = jnp.dot(flat_tokens, projection, preferred_element_type=jnp.float32)
    bias_values = proj_bias.astype(jnp.float32)
    queries = (
        (projected[:, :D] + bias_values[0]).astype(jnp.bfloat16).reshape(row_count, block_len, D)
    )
    keys_own = projected[:, D : 2 * D].astype(jnp.bfloat16).reshape(row_count, block_len, D)
    values_own = (
        (projected[:, 2 * D :] + bias_values[1])
        .astype(jnp.bfloat16)
        .reshape(row_count, block_len, D)
    )
    doc_len = jnp.where(row_kinds == 0, DOC_SHORT, length).astype(jnp.int32)
    first_pos = lax.axis_index("blk") * block_len
    query_seg = (first_pos + jnp.arange(block_len, dtype=jnp.int32))[None, :] // doc_len[:, None]
    key_seg = jnp.arange(length, dtype=jnp.int32)[None, :] // doc_len[:, None]
    live_low = live_mask.astype(jnp.bfloat16)
    keys_all, values_all, live_all = (
        lax.all_gather(keys_own, "blk", axis=1, tiled=True),
        lax.all_gather(values_own, "blk", axis=1, tiled=True),
        lax.all_gather(live_low, "blk", axis=1, tiled=True),
    )
    attended, log_total = lax.map(
        attend_row, (queries, keys_all, values_all, query_seg, key_seg, live_all)
    )
    attended_flat = attended.reshape(row_count * block_len, D)
    attn_out = jnp.dot(attended_flat, mixing, preferred_element_type=jnp.float32) + mix_bias.astype(
        jnp.float32
    )
    normed, norm_one_back = jax.vjp(
        layer_norm,
        token_values + attn_out,
        attn_gain.astype(jnp.float32),
        attn_shift.astype(jnp.float32),
    )
    normed_low = normed.astype(jnp.bfloat16)
    pre_act = jnp.dot(normed_low, expand, preferred_element_type=jnp.float32) + expand_bias.astype(
        jnp.float32
    )
    gelu_value, gelu_back = jax.vjp(partial(jax.nn.gelu, approximate=False), pre_act)
    activated = gelu_value.astype(jnp.bfloat16)
    ffn_out = jnp.dot(
        activated, contract, preferred_element_type=jnp.float32
    ) + contract_bias.astype(jnp.float32)
    normed_two, norm_two_back = jax.vjp(
        layer_norm, normed + ffn_out, ffn_gain.astype(jnp.float32), ffn_shift.astype(jnp.float32)
    )
    keep_tokens = jnp.broadcast_to(keep_flag[:, None], (row_count, block_len)).reshape(-1, 1) > 0
    layer_out = jnp.where(keep_tokens, normed_two, token_values).astype(jnp.bfloat16)
    cotangent_flat = cotangent.reshape(row_count * block_len, D).astype(jnp.float32)
    grad_two = cotangent_flat * keep_tokens.astype(jnp.float32)
    d_resid_two, ffn_gain_grad, ffn_shift_grad = norm_two_back(grad_two)
    d_ffn = d_resid_two.astype(jnp.bfloat16)
    contract_grad = jnp.dot(activated.T, d_ffn, preferred_element_type=jnp.float32)
    contract_bias_grad = jnp.sum(d_ffn.astype(jnp.float32), axis=0)
    d_act = jnp.dot(d_ffn, contract.T, preferred_element_type=jnp.float32)
    d_pre = gelu_back(d_act)[0].astype(jnp.bfloat16)
    expand_grad = jnp.dot(normed_low.T, d_pre, preferred_element_type=jnp.float32)
    expand_bias_grad = jnp.sum(d_pre.astype(jnp.float32), axis=0)
    ffn_group = (
        expand_grad,
        expand_bias_grad,
        contract_grad,
        contract_bias_grad,
        ffn_gain_grad,
        ffn_shift_grad,
    )
    d_normed = d_resid_two + jnp.dot(d_pre, expand.T, preferred_element_type=jnp.float32)
    d_resid_one, attn_gain_grad, attn_shift_grad = norm_one_back(d_normed)
    d_attn = d_resid_one.astype(jnp.bfloat16)
    mixing_grad = jnp.dot(attended_flat.T, d_attn, preferred_element_type=jnp.float32)
    mix_bias_grad = jnp.sum(d_attn.astype(jnp.float32), axis=0)
    d_attended = jnp.dot(d_attn, mixing.T, preferred_element_type=jnp.float32).astype(jnp.bfloat16)
    d_attended = d_attended.reshape(row_count, block_len, D)
    keys_back, values_back, live_back = (
        lax.all_gather(keys_own, "blk", axis=1, tiled=True),
        lax.all_gather(values_own, "blk", axis=1, tiled=True),
        lax.all_gather(live_low, "blk", axis=1, tiled=True),
    )
    d_queries, deltas, key_terms, value_terms = lax.map(
        partial(query_grad_row, True),
        (queries, keys_back, values_back, query_seg, key_seg, live_back, log_total, d_attended),
    )
    d_keys, d_values = (
        lax.psum_scatter(
            key_terms.astype(jnp.bfloat16), "blk", scatter_dimension=1, tiled=True
        ).astype(jnp.float32),
        lax.psum_scatter(
            value_terms.astype(jnp.bfloat16), "blk", scatter_dimension=1, tiled=True
        ).astype(jnp.float32),
    )
    d_projected = jnp.concatenate(
        [d_queries, d_keys.astype(jnp.bfloat16), d_values.astype(jnp.bfloat16)], axis=-1
    ).reshape(row_count * block_len, 3 * D)
    projection_grad = jnp.dot(flat_tokens.T, d_projected, preferred_element_type=jnp.float32)
    proj_bias_grad = jnp.stack(
        [
            jnp.sum(d_projected[:, :D].astype(jnp.float32), axis=0),
            jnp.sum(d_projected[:, 2 * D :].astype(jnp.float32), axis=0),
        ]
    )
    d_tokens = d_resid_one + jnp.dot(d_projected, projection.T, preferred_element_type=jnp.float32)
    tokens_grad = jnp.where(keep_tokens, d_tokens, cotangent_flat).reshape(row_count, block_len, D)
    attn_group = (
        projection_grad,
        proj_bias_grad,
        mixing_grad,
        mix_bias_grad,
        attn_gain_grad,
        attn_shift_grad,
    )
    summed = lax.psum(attn_group + ffn_group, ("dp", "blk"))
    attn_group = summed[:6]
    ffn_group = summed[6:]
    return (
        layer_out.reshape(row_count, block_len, D),
        tokens_grad,
        attn_group[0],
        attn_group[1],
        attn_group[2],
        attn_group[3],
        attn_group[4],
        attn_group[5],
        ffn_group[0],
        ffn_group[1],
        ffn_group[2],
        ffn_group[3],
        ffn_group[4],
        ffn_group[5],
    )


def solution(mesh):
    in_specs = (
        P("dp", "blk", None),
        P("dp"),
        P("dp", "blk"),
        P("dp"),
        P(),
        P(),
        P(),
        P(),
        P(),
        P(),
        P(),
        P(),
        P(),
        P(),
        P(),
        P(),
        P("dp", "blk", None),
    )
    out_specs = (
        P("dp", "blk", None),
        P("dp", "blk", None),
        P(),
        P(),
        P(),
        P(),
        P(),
        P(),
        P(),
        P(),
        P(),
        P(),
        P(),
        P(),
    )
    return jax.shard_map(local, mesh=mesh, in_specs=in_specs, out_specs=out_specs, check_vma=False)
```

profile of v0, /device:TPU:0, one launch (start us, length us, event | category | flops | bytes accessed | tf_op | source)
XLA Modules:
  0.0 918.3 jit_solution(16060989639696876011)
XLA Ops:
  34.2 15.3 %all_gather.13 = bf16[4,512]{1,0:T(4,128)(2,1)} all-gather(bf16[4,128]{1,0:T(4,128)(2,1)S(1)} %convert_element_type.148), channel_id=1, replica_groups=mesh['dp'=8,'blk'=4] {'blk'}, dimensions={1}, use_global_device_ids=true | all-gather | bytes 5120 | tf_op jit(solution)/shard_map/all_gather | solution.py:127
  53.6 30.5 %all-gather.5.cloned.1.call-done = bf16[4,512,768]{1,2,0:T(8,128)(2,1)} async-done(((bf16[4,128,768]{1,2,0:T(8,128)(2,1)}), bf16[4,512,768]{1,2,0:T(8,128)(2,1)}) %all-gather.5.cloned.1.call-update) | async-done | bytes 3145744 | tf_op jit(solution)/shard_map/all_gather | solution.py:125
  84.1 63.8 %all-gather.3.cloned.1.call-done = bf16[4,512,768]{1,2,0:T(8,128)(2,1)} async-done(((bf16[4,128,768]{1,2,0:T(8,128)(2,1)}), bf16[4,512,768]{1,2,0:T(8,128)(2,1)}) %all-gather.3.cloned.1.call-update) | async-done | bytes 3145744 | tf_op jit(solution)/shard_map/all_gather | solution.py:126
  147.9 49.0 %while.26 = (s32[]{:T(128)}, bf16[4,128,768]{2,1,0:T(8,128)(2,1)}, f32[4,12,128]{2,1,0:T(8,128)}, bf16[4,512,768]{1,2,0:T(8,128)(2,1)}, s32[4,128]{1,0:T(4,128)}...) while((s32[]{:T(128)}, bf16[4,128,768]{2,1,0:T(8,128)(2,1)}, ...), condition=%wide.region_3.4_spmd, body=%wide.region_0.3_spmd.sunk | while | flops 210993152 | bytes 16051849 | solution.py:129
  200.1 19.6 %multiply_convert_fusion.1 = (bf16[512,3072]{1,0:T(8,128)(2,1)S(1)}, f32[512,3072]{1,0:T(8,128)}, f32[512,3072]{1,0:T(8,128)}) fusion(f32[3072]{0:T(1024)S(1)} %copy-done.18, bf16[768,3072]{1,0:T(8,128)(2,1)} %param.31, f32[512,768]{1,0:T(8,128)S(1)} %get-tuple-element.329, f32[768]{0:T(1024)S(1)} %copy-done.23, f32[768]{0:T(1024)S(1)} %copy-done.15, ...), kind=kOutput, calls=%fused_computation.46 | convolution fusion | flops 2521694208 | bytes 22042624 | tf_op jit(solution)/shard_map/dot_general | solution.py:143
  226.6 9.9 %convert_reduce_fusion = (f32[3072]{0:T(1024)}, bf16[512,3072]{1,0:T(8,128)(2,1)}) fusion(f32[512,3072]{1,0:T(8,128)} %get-tuple-element.310, f32[512,3072]{1,0:T(8,128)} %get-tuple-element.330, f32[3072]{0:T(1024)S(1)} %copy-done.18, bf16[512,768]{1,0:T(8,128)(2,1)S(1)} %get-tuple-element.300, bf16[3072,768]{1,0:T(8,128)(2,1)S(1)} %bitcast.201), kind=kOutput, calls=%fused_computation.44 | convolution fusion | flops 2442654720 | bytes 21258240 | tf_op jit(solution)/shard_map/dot_general | solution.py:162
  236.4 5.6 multiply_reduce_fusion.1
  247.3 63.8 %while.27 = (s32[]{:T(128)}, bf16[4,128,768]{1,2,0:T(8,128)(2,1)}, bf16[4,512,768]{1,2,0:T(8,128)(2,1)}, bf16[4,512,768]{1,2,0:T(8,128)(2,1)}, bf16[4,512,768]{1...) while((s32[]{:T(128)}, bf16[4,128,768]{1,2,0:T(8,128)(2,1)}, ...), condition=%wide.region_14.15_spmd, body=%wide.region_12.14_spmd.sunk | while | flops 511508480 | bytes 37592804 | solution.py:186
  311.1 6.0 copy.55
  317.0 4.2 copy.61
  321.4 6.1 copy.53
  327.5 4.2 copy.60
  335.6 5.5 fusion.47
  341.1 5.6 fusion.35
  346.7 33.2 %reduce-scatter.9.cloned.1.call-done = bf16[128,3072]{1,0:T(8,128)(2,1)} async-done(((bf16[512,3072]{1,0:T(8,128)(2,1)}), bf16[128,3072]{1,0:T(8,128)(2,1)}) %reduce-scatter.9.cloned.1.call-update) | async-done | bytes 786448
  384.7 57.6 %reduce-scatter.7.cloned.1.call-done = bf16[128,3072]{1,0:T(8,128)(2,1)} async-done(((bf16[512,3072]{1,0:T(8,128)(2,1)}), bf16[128,3072]{1,0:T(8,128)(2,1)}) %reduce-scatter.7.cloned.1.call-update) | async-done | bytes 786448
  447.2 6.8 convolution_bitcast_fusion
  459.8 4.6 copy.51
  466.0 43.9 %all-reduce = (f32[2,768]{1,0:T(2,128)}, f32[768]{0:T(1024)}, f32[768]{0:T(1024)}, f32[768]{0:T(1024)}, f32[3072]{0:T(1024)}, /*index=5*/f32[768]{0:T(1024)}, f32[768]{0:T(1024)}, f32[768]{0:T(1024)}) all-reduce(f32[2,768]{1,0:T(2,128)S(1)} %pad_maximum_fusion.1, ...), channel_id=1, replica_groups=mesh['dp'=8,'blk'=4] {'dp','blk'}, use_global_device_ids=true, to_apply=%region_20.21 | all-reduce | flops 9216 | bytes 73728 | tf_op jit(solution)/shard_map/psum | solution.py:218
  510.0 5.7 bitcast_select_fusion
  515.6 371.8 %all-reduce.4.cloned.1.call-done = (f32[768,2304]{0,1:T(8,128)}, f32[768,768]{1,0:T(8,128)}, f32[768,3072]{1,0:T(8,128)}, f32[3072,768]{1,0:T(8,128)}) async-done(((f32[768,2304]{0,1:T(8,128)}, f32[768,768]{1,0:T(8,128)}, f32[768,3072]{1,0:T(8,128)}, f32[3072,768]{1,0:T(8,128)}), (f32[768,2304]{0,1:T(8,128)}, f32[768,768]{1,0:T(8,128)}, f32[768,3072]{1,0:T(8,128)}, ...) | async-done | bytes 28311568 | tf_op jit(solution)/shard_map/psum | solution.py:218
  887.5 8.0 copy.52
  898.8 8.8 copy.99
  907.6 3.7 copy.100
  (285 shorter events, 182.8 us)
Async XLA Ops:
  7.2 76.9 %all-gather.5.cloned.1.call-start = ((), (), s32[]{:S(2)}) async-start(), calls=%async_computation.3 | async-start | bytes 3932160 | tf_op jit(solution)/shard_map/all_gather | solution.py:125
  17.8 130.1 %all-gather.3.cloned.1.call-start = ((), (), s32[]{:S(2)}) async-start(), calls=%async_computation.2 | async-start | bytes 3932160 | tf_op jit(solution)/shard_map/all_gather | solution.py:126
  17.9 6.4 copy-start.27
  17.9 13.4 %copy-start.22 = (bf16[3072]{0:T(1024)(128)(2,1)S(1)}, bf16[3072]{0:T(1024)(128)(2,1)}, u32[]{:S(2)}) copy-start(bf16[3072]{0:T(1024)(128)(2,1)} %param.32) | copy-start | bytes 18436
  23.5 356.4 %reduce-scatter.9.cloned.1.call-start = ((), (), s32[]{:S(2)}) async-start(), calls=%async_computation.5 | async-start | bytes 3932160
  196.9 22.8 %slice-start.3 = ((s8[4718592]{0:T(1024)(128)(4,1)}), s8[4194304]{0:T(1024)(128)(4,1)S(1)}, s32[]{:S(2)}) async-start(s8[4718592]{0:T(1024)(128)(4,1)} %bitcast.200), calls=%async_computation.10 | async-start | bytes 8388608
  199.7 42.4 %copy-start.4 = (f32[512,768]{1,0:T(8,128)}, f32[512,768]{1,0:T(8,128)S(1)}, u32[]{:S(2)}) copy-start(f32[512,768]{1,0:T(8,128)S(1)} %get-tuple-element.329) | copy-start | bytes 4718596
  200.1 42.1 %copy-start.19 = (f32[512]{0:T(512)}, f32[512]{0:T(512)S(1)}, u32[]{:S(2)}) copy-start(f32[512]{0:T(512)S(1)} %fusion.30) | copy-start | bytes 6148
  200.1 19.6 %copy-start.25 = (f32[768]{0:T(1024)S(1)}, f32[768]{0:T(1024)}, u32[]{:S(2)}) copy-start(f32[768]{0:T(1024)} %convert_element_type.156) | copy-start | bytes 9220
  200.1 19.6 %slice-start.4 = ((s8[4718592]{0:T(1024)(128)(4,1)}), s8[524288]{0:T(1024)(128)(4,1)S(1)}, s32[]{:S(2)}) async-start(s8[4718592]{0:T(1024)(128)(4,1)} %bitcast.200), calls=%async_computation.11 | async-start | bytes 1048576
  223.7 12.7 %slice-start.5 = ((s8[4718592]{0:T(1024)(128)(4,1)}), s8[4194304]{0:T(1024)(128)(4,1)S(1)}, s32[]{:S(2)}) async-start(s8[4718592]{0:T(1024)(128)(4,1)} %bitcast.202), calls=%async_computation.12 | async-start | bytes 8388608
  226.6 9.9 %copy-start.9 = (bf16[512,768]{1,0:T(8,128)(2,1)}, bf16[512,768]{1,0:T(8,128)(2,1)S(1)}, u32[]{:S(2)}) copy-start(bf16[512,768]{1,0:T(8,128)(2,1)S(1)} %get-tuple-element.300) | copy-start | bytes 2359300
  226.6 9.9 %slice-start.6 = ((s8[4718592]{0:T(1024)(128)(4,1)}), s8[524288]{0:T(1024)(128)(4,1)S(1)}, s32[]{:S(2)}) async-start(s8[4718592]{0:T(1024)(128)(4,1)} %bitcast.202), calls=%async_computation.13 | async-start | bytes 1048576
  321.3 121.0 %reduce-scatter.7.cloned.1.call-start = ((), (), s32[]{:S(2)}) async-start(), calls=%async_computation.4 | async-start | bytes 3932160
  331.7 555.7 %all-reduce.4.cloned.1.call-start = ((), (), s32[]{:S(2)}) async-start(), calls=%async_computation.6 | async-start | bytes 56623104 | tf_op jit(solution)/shard_map/psum | solution.py:218
  335.6 5.5 copy-start.5
  335.6 5.5 copy-start.16
  335.6 5.5 copy-start.20
  335.6 5.5 copy-start.24
  335.6 5.5 copy-start.33
  459.8 6.2 copy-start.14
  895.4 12.1 %slice-start = ((s8[9437184]{0:T(1024)(128)(4,1)}), s8[4194304]{0:T(1024)(128)(4,1)S(1)}, s32[]{:S(2)}) async-start(s8[9437184]{0:T(1024)(128)(4,1)} %bitcast.182), calls=%async_computation.7 | async-start | bytes 8388608
  898.8 8.8 slice-start.1
  898.8 8.8 slice-start.2
  (28 other events, 72.0 us)
Sparse Core Ops, SparseCore 0:
  17.9 66.1 all-gather.4
  86.3 61.5 all-gather.2
  321.4 58.3 reduce-scatter.8
  382.0 60.2 reduce-scatter.6
  454.1 433.2 all-reduce.3
where the time goes:
time: 924 us; the launch traced here: 918 us
  waiting for transfers between devices  557 us (60%)
  local copies, waits for them, and re-layouts  145 us (16%)
  matrix products  97.1 us (11%)
  blocking collectives  59.2 us (6%)
  other arithmetic  44.5 us (5%)
  between operations  14.7 us (2%)
    psum x1, waiting for transfers between devices, local(): summed = lax.psum(attn_group + ffn_group, ('dp', 'blk'))  372 us
    unnamed x7, waiting for transfers between devices  90.9 us
    all_gather x1, waiting for transfers between devices, local(): lax.all_gather(values_own, 'blk', axis=1, tiled=True)  63.8 us
    unnamed x90, local copies, waits for them, and re-layouts  61 us
    psum x1, blocking collectives, local(): summed = lax.psum(attn_group + ffn_group, ('dp', 'blk'))  43.9 us
    dynamic_slice x36, local copies, waits for them, and re-layouts, local(): lax.map(attend_row, (queries, keys_all, values_all, query_seg, key_seg, l...  42.3 us
    all_gather x1, waiting for transfers between devices, local(): lax.all_gather(keys_own, 'blk', axis=1, tiled=True)  30.5 us
    dot_general x1, matrix products, local(): jnp.dot(normed_low, expand, preferred_element_type=jnp.float32)  19.6 us
  transfers between devices with their start and end apart: 5, of which 5 were waited for; matrix products, arithmetic and copies ran while one was open for 7% of the time, Pallas kernels for 0%

commit v1 on v0

v1 whole, which is shorter than its diff:
```python
import functools
import jax
import jax.numpy as jnp
from jax import lax
from jax.experimental import pallas as pl
from jax.experimental.pallas import tpu as pltpu
from jax.sharding import PartitionSpec as P

D = 768
HEADS = 12
HEAD_DIM = 64
DOC_SHORT = 128
MESH = pl.DeviceIdType.MESH
norm_eps = 1e-05
NEG = -1e9
F32, B16 = jnp.float32, jnp.bfloat16
NN = (((1,), (0,)), ((), ()))
NT = (((1,), (1,)), ((), ()))
TN = (((0,), (0,)), ((), ()))
def dot(a, b, dims=NN):
    return lax.dot_general(a, b, dims, preferred_element_type=F32)

def fwd_kernel(q, k, v, bias, att, probs):
    for h in range(2):
        s = slice(h * HEAD_DIM, (h + 1) * HEAD_DIM)
        scores = dot(q[:, s] * jnp.asarray(HEAD_DIM ** -0.5, B16), k[:, s], NT) + bias[...]
        top = jnp.max(scores, axis=1, keepdims=True)
        e = jnp.exp(scores - top)
        p = (e * (1.0 / jnp.sum(e, axis=1, keepdims=True))).astype(B16)
        probs[h] = p
        att[:, s] = dot(p, v[:, s]).astype(B16)

def attend(qkv, bias):
    T = qkv.shape[0]
    W = 2 * HEAD_DIM
    G = HEADS // 2
    col = lambda off: pl.BlockSpec((T, W), lambda i: (0, off + i))
    return pl.pallas_call(fwd_kernel, grid=(G,),
        in_specs=[col(0), col(G), col(2 * G), pl.BlockSpec((T, T), lambda i: (0, 0))],
        out_specs=[col(0), pl.BlockSpec((2, T, T), lambda i: (i, 0, 0))],
        out_shape=[jax.ShapeDtypeStruct((T, D), B16), jax.ShapeDtypeStruct((HEADS, T, T), B16)],
        compiler_params=pltpu.CompilerParams(vmem_limit_bytes=48 * 2**20),
        cost_estimate=pl.CostEstimate(flops=4 * T * T * D * 4, bytes_accessed=20 * 2**20, transcendentals=HEADS * T * T),
        name="attend")(qkv, qkv, qkv, bias)

def bwd_kernel(q, k, v, probs, da, dq, dk, dv):
    scale = HEAD_DIM ** -0.5
    for h in range(2):
        s = slice(h * HEAD_DIM, (h + 1) * HEAD_DIM)
        dah = da[:, s]
        p = probs[h]
        dp = dot(dah, v[:, s], NT)
        pf = p.astype(F32)
        delta = jnp.sum(pf * dp, axis=1, keepdims=True)
        ds = (pf * (dp - delta)).astype(B16)
        dq[:, s] = (dot(ds, k[:, s]) * scale).astype(B16)
        dk[:, s] = (dot(q[:, s], ds, TN) * scale).T.astype(B16)
        dv[:, s] = dot(dah, p, TN).T.astype(B16)

def attend_back(qkv, probs, da):
    T = qkv.shape[0]
    W = 2 * HEAD_DIM
    G = HEADS // 2
    col = lambda off: pl.BlockSpec((T, W), lambda i: (0, off + i))
    return pl.pallas_call(bwd_kernel, grid=(G,),
        in_specs=[col(0), col(G), col(2 * G), pl.BlockSpec((2, T, T), lambda i: (i, 0, 0)), col(0)],
        out_specs=[col(0)] * 3,
        out_shape=[jax.ShapeDtypeStruct((T, D), B16)] * 3,
        compiler_params=pltpu.CompilerParams(vmem_limit_bytes=48 * 2**20),
        cost_estimate=pl.CostEstimate(flops=8 * T * T * D * 4, bytes_accessed=20 * 2**20, transcendentals=0),
        name="attend_back")(qkv, qkv, qkv, probs, da)


CR, CC = 384, 768
HR, HC = CR // 2, CC // 2
SR = HR // 4
N = 24
KINDS = 12
OFF = [0, 1, 4, 6, 8, 10, 12, 14, 16, 18, 21, 22]
CORE, FIRST, ZA, ZB, ZC, LAST, GR, GL, GF, GE, AGF, AGC = range(KINDS)

def grads_kernel(act, d_ffn, low, d_pre, att, d_att, tok, d_proj, small, g_out, small_out,
           part, r0, r1, za, zb, zc, ry, fin, sm, smr, ssem, rsem, lsem, smss, smrs):
    dp, z = lax.axis_index("dp"), lax.axis_index("blk")
    c, x, y = dp % 2, (dp // 2) % 2, (dp // 4) % 2
    d_core = (dp + 1 - 2 * c, z)
    d_x = (dp + 2 - 4 * x, z)
    d_y = (dp + 4 - 8 * y, z)
    right, left = (dp, jnp.minimum(z + 1, 3)), (dp, jnp.maximum(z - 1, 0))
    is0, is1, is2, is3 = z == 0, z == 1, z == 2, z == 3
    end, mid = (z == 0) | (z == 3), (z == 1) | (z == 2)

    barrier = pltpu.get_barrier_semaphore()
    for d in (d_core, d_x, d_y):
        pl.semaphore_signal(barrier, inc=1, device_id=d, device_id_type=MESH)
    @pl.when(z < 3)
    def _():
        pl.semaphore_signal(barrier, inc=1, device_id=right, device_id_type=MESH)
    @pl.when(z > 0)
    def _():
        pl.semaphore_signal(barrier, inc=1, device_id=left, device_id_type=MESH)
    pl.semaphore_wait(barrier, jnp.where(end, 4, 5))

    def cp(kind, k, src, dst, dev):
        return pltpu.make_async_remote_copy(src_ref=src, dst_ref=dst, send_sem=ssem.at[kind, k],
            recv_sem=rsem.at[kind, k], device_id=dev, device_id_type=MESH)

    def ctx(k):
        par = k % 2
        f = x * (1 - par) + y * par
        d_first = (dp + (1 - par) * (2 - 4 * x) + par * (4 - 8 * y), z)
        d_last = (dp + par * (2 - 4 * x) + (1 - par) * (4 - 8 * y), z)
        return f, d_first, d_last

    def rows(start, n):
        return pl.ds(pl.multiple_of(start, 16), n)
    def cols(start, n):
        return pl.ds(pl.multiple_of(start, 128), n)
    keep = rows(c * HR, HR)
    give = rows((1 - c) * HR, HR)

    def c_core(k):
        return cp(CORE, k, part.at[k % 2, give], r0.at[k], d_core)
    def c_first(k):
        f, d_first, _ = ctx(k)
        return cp(FIRST, k, r0.at[k, :, cols((1 - f) * HC, HC)], r1.at[k], d_first)
    def c_za(k):
        src = r1.at[k, rows(jnp.where(is0, SR, 0), 3 * SR)]
        return cp(ZA, k, src, za.at[k], (dp, jnp.where(is0, 1, 2)))
    def c_zb(k):
        src = r1.at[k, rows(jnp.where(is1, 2 * SR, 0), 2 * SR)]
        return cp(ZB, k, src, zb.at[k], (dp, jnp.where(is1, 2, 1)))
    def c_zc(k):
        src = r1.at[k, rows(jnp.where(is1, 0, 3 * SR), SR)]
        return cp(ZC, k, src, zc.at[k], (dp, jnp.where(is1, 0, 3)))
    def c_last(k):
        _, _, d_last = ctx(k)
        return cp(LAST, k, r1.at[k, rows(z * SR, SR)], ry.at[k], d_last)
    def place(k, shard, n=1):
        f, _, _ = ctx(k)
        return g_out.at[k, rows(c * HR + shard * SR, n * SR), cols(f * HC, HC)]
    def c_gr(k):
        return cp(GR, k, fin.at[k], place(k, z), right)
    def c_gl(k):
        return cp(GL, k, fin.at[k], place(k, z), left)
    def c_own(k):
        return pltpu.make_async_copy(fin.at[k], place(k, z), lsem.at[k])
    def c_gf(k):
        s = jnp.where(is1, 0, 3)
        return cp(GF, k, place(k, s), place(k, s), (dp, jnp.where(is1, 2, 1)))
    def c_ge(k):
        s = jnp.where(is1, 2, 0)
        return cp(GE, k, place(k, s, 2), place(k, s, 2), (dp, jnp.where(is1, 0, 3)))
    def c_agf(k):
        f, d_first, _ = ctx(k)
        blk = g_out.at[k, keep, cols(f * HC, HC)]
        return cp(AGF, k, blk, blk, d_first)
    def c_agc(k):
        blk = g_out.at[k, keep]
        return cp(AGC, k, blk, blk, d_core)

    def add(a, b):
        return (a.astype(jnp.float32) + b.astype(jnp.float32)).astype(jnp.bfloat16)

    def produce(k):
        def dot(l, lc, r, rc):
            return lax.dot_general(l[:, cols(lc * CR, CR)], r[:, cols(rc * CC, CC)], (((0,), (0,)), ((), ())),
                                   preferred_element_type=jnp.float32).astype(jnp.bfloat16)
        @pl.when(k < 8)
        def _():
            part[k % 2] = dot(act, k, d_ffn, 0)
        @pl.when((k >= 8) & (k < 16))
        def _():
            j = k - 8
            part[k % 2] = dot(low, j // 4, d_pre, j % 4)
        @pl.when((k >= 16) & (k < 18))
        def _():
            part[k % 2] = dot(att, k - 16, d_att, 0)
        @pl.when(k >= 18)
        def _():
            j = k - 18
            part[k % 2] = dot(tok, j // 3, d_proj, j % 3)

    def stage(s, k):
        if s == 0:
            @pl.when(k >= 2)
            def _(): c_core(k - 2).wait_send()
            produce(k)
            c_core(k).start()
        elif s == 1:
            c_core(k).wait_recv()
            r0[k] = add(r0[k], part[k % 2, keep])
            c_first(k).start()
        elif s == 2:
            f, _, _ = ctx(k)
            c_first(k).wait_recv()
            r1[k] = add(r1[k], r0[k, :, cols(f * HC, HC)])
            @pl.when(end)
            def _(): c_za(k).start()
        elif s == 3:
            @pl.when(mid)
            def _():
                c_za(k).wait_recv()
                own = rows(jnp.where(is1, SR, 0), 3 * SR)
                r1[k, own] = add(r1[k, own], za[k])
                c_zb(k).start()
        elif s == 4:
            @pl.when(mid)
            def _():
                c_zb(k).wait_recv()
                own = rows(jnp.where(is1, 0, 2 * SR), 2 * SR)
                r1[k, own] = add(r1[k, own], zb[k])
                c_zc(k).start()
        elif s == 5:
            @pl.when(end)
            def _():
                c_zc(k).wait_recv()
                own = rows(z * SR, SR)
                r1[k, own] = add(r1[k, own], zc[k])
            c_last(k).start()
        elif s == 6:
            c_last(k).wait_recv()
            fin[k] = add(r1[k, rows(z * SR, SR)], ry[k])
            c_own(k).start()
            @pl.when(z < 3)
            def _(): c_gr(k).start()
            @pl.when(z > 0)
            def _(): c_gl(k).start()
        elif s == 7:
            @pl.when(is1)
            def _(): c_gr(k).wait_recv()
            @pl.when(is2)
            def _(): c_gl(k).wait_recv()
            @pl.when(mid)
            def _(): c_gf(k).start()
        elif s == 8:
            @pl.when(is1)
            def _(): c_gl(k).wait_recv()
            @pl.when(is2)
            def _(): c_gr(k).wait_recv()
            @pl.when(mid)
            def _():
                c_gf(k).wait_recv()
                c_ge(k).start()
        elif s == 9:
            @pl.when(is0)
            def _(): c_gl(k).wait_recv()
            @pl.when(is3)
            def _(): c_gr(k).wait_recv()
            @pl.when(end)
            def _(): c_ge(k).wait_recv()
            c_own(k).wait()
            c_agf(k).start()
        elif s == 10:
            c_agf(k).wait_recv()
            c_agc(k).start()
        elif s == 11:
            c_agc(k).wait_recv()
            c_first(k).wait_send()
            c_last(k).wait_send()
            @pl.when(end)
            def _(): c_za(k).wait_send()
            @pl.when(mid)
            def _():
                c_zb(k).wait_send()
                c_zc(k).wait_send()
                c_gf(k).wait_send()
                c_ge(k).wait_send()
            @pl.when(z < 3)
            def _(): c_gr(k).wait_send()
            @pl.when(z > 0)
            def _(): c_gl(k).wait_send()
            c_agf(k).wait_send()
            c_agc(k).wait_send()

    def s_copy(i):
        dev = (d_core, d_x, d_y, (dp, jnp.where(is0, 1, 2)), (dp, jnp.where(is1, 2, 1)), (dp, jnp.where(is1, 0, 3)))[i]
        return pltpu.make_async_remote_copy(src_ref=sm.at[i], dst_ref=smr.at[i], send_sem=smss.at[i], recv_sem=smrs.at[i],
            device_id=dev, device_id_type=MESH)
    sm[0] = small[...]
    def s_step(i):
        if i > 0:
            sends = (None, None, None, end, mid, mid)[i - 1]
            gets = (None, None, None, mid, mid, end)[i - 1]
            def get():
                s_copy(i - 1).wait_recv()
                if i == 6:
                    sm[i] = smr[i - 1]
                else:
                    sm[i] = sm[i - 1] + smr[i - 1]
            if gets is None:
                get()
            else:
                pl.when(gets)(get)
                @pl.when(jnp.logical_not(gets))
                def _(): sm[i] = sm[i - 1]
        if i < 6:
            sends = (None, None, None, end, mid, mid)[i]
            if sends is None:
                s_copy(i).start()
            else:
                pl.when(sends)(lambda: s_copy(i).start())

    def tick(t, _):
        for s in range(len(OFF) - 1, -1, -1):
            k = t - OFF[s]
            @pl.when((k >= 0) & (k < N))
            def _():
                stage(s, k)
        for i in range(7):
            @pl.when(t == N + i)
            def _():
                s_step(i)
        return 0
    lax.fori_loop(0, N + OFF[-1], tick, 0)
    for i in range(6):
        sends = (None, None, None, end, mid, mid)[i]
        if sends is None:
            s_copy(i).wait_send()
        else:
            pl.when(sends)(lambda: s_copy(i).wait_send())
    @pl.when(mid)
    def _(): small_out[...] = sm[5]
    @pl.when(end)
    def _(): small_out[...] = sm[6]
    for k in (N - 2, N - 1):
        c_core(k).wait_send()

def sum_grads(act, d_ffn, low, d_pre, att, d_att, tok, d_proj, small):
    B = jnp.bfloat16
    V = pl.BlockSpec(memory_space=pltpu.VMEM)
    return pl.pallas_call(grads_kernel,
        out_shape=[jax.ShapeDtypeStruct((N, CR, CC), B), jax.ShapeDtypeStruct(small.shape, jnp.float32)],
        in_specs=[V] * 9,
        out_specs=[pl.BlockSpec(memory_space=pltpu.HBM), V],
        scratch_shapes=[
            pltpu.VMEM((2, CR, CC), B), pltpu.VMEM((N, HR, CC), B), pltpu.VMEM((N, HR, HC), B),
            pltpu.VMEM((N, 3 * SR, HC), B), pltpu.VMEM((N, 2 * SR, HC), B), pltpu.VMEM((N, SR, HC), B),
            pltpu.VMEM((N, SR, HC), B), pltpu.VMEM((N, SR, HC), B),
            pltpu.VMEM((7,) + small.shape, jnp.float32), pltpu.VMEM((6,) + small.shape, jnp.float32),
            pltpu.SemaphoreType.DMA((KINDS, N)), pltpu.SemaphoreType.DMA((KINDS, N)), pltpu.SemaphoreType.DMA((N,)),
            pltpu.SemaphoreType.DMA((6,)), pltpu.SemaphoreType.DMA((6,)),
        ],
        compiler_params=pltpu.CompilerParams(collective_id=0, has_side_effects=True, vmem_limit_bytes=60 * 2**20),
        name="grads",
    )(act, d_ffn, low, d_pre, att, d_att, tok, d_proj, small)


def deal(blocks):
    z = lax.axis_index("blk")
    n = blocks.shape[0]
    out = jnp.zeros_like(blocks)
    for m in range(n):
        piece = lax.dynamic_index_in_dim(blocks, z ^ m, 0)
        if m:
            piece = lax.ppermute(piece, "blk", [(i, i ^ m) for i in range(n)])
        out = lax.dynamic_update_slice(out, piece, (z ^ m,) + (0,) * (blocks.ndim - 1))
    return out


def layer_norm(hidden, gain_vec, shift_vec):
    row_mean = jnp.mean(hidden, axis=-1, keepdims=True)
    centered = hidden - row_mean
    variance = jnp.mean(centered * centered, axis=-1, keepdims=True)
    return centered * lax.rsqrt(variance + norm_eps) * gain_vec + shift_vec


def local(tokens, row_kinds, live_mask, keep_flag, projection, proj_bias, mixing, mix_bias, attn_gain, attn_shift,
          expand, expand_bias, contract, contract_bias, ffn_gain, ffn_shift, cotangent):
    row_count, block_len, _ = tokens.shape
    blocks = lax.axis_size("blk")
    length = block_len * blocks
    z = lax.axis_index("blk")
    f32 = lambda a: a.astype(F32)
    row = deal(tokens).reshape(length, D)
    live = deal(live_mask[:, None]).reshape(length)
    cot = deal(cotangent).reshape(length, D)
    kind = lax.dynamic_index_in_dim(row_kinds, z, 0, False)
    keep = lax.dynamic_index_in_dim(keep_flag, z, 0, False) > 0

    seg = jnp.arange(length, dtype=jnp.int32) // jnp.where(kind == 0, DOC_SHORT, length)
    allowed = (seg[:, None] == seg[None, :]) & (live[None, :] > 0)
    bias = jnp.where(allowed, 0.0, NEG).astype(F32)
    qkv_bias = jnp.concatenate([f32(proj_bias[0]), jnp.zeros((D,), F32), f32(proj_bias[1])])
    qkv = (dot(row, projection) + qkv_bias).astype(B16)
    attended, probs = attend(qkv, bias)

    attn_out = dot(attended, mixing) + f32(mix_bias)
    normed, norm_one_back = jax.vjp(layer_norm, f32(row) + attn_out, f32(attn_gain), f32(attn_shift))
    normed_low = normed.astype(B16)
    pre_act = dot(normed_low, expand) + f32(expand_bias)
    gelu_value, gelu_back = jax.vjp(functools.partial(jax.nn.gelu, approximate=False), pre_act)
    activated = gelu_value.astype(B16)
    ffn_out = dot(activated, contract) + f32(contract_bias)
    normed_two, norm_two_back = jax.vjp(layer_norm, normed + ffn_out, f32(ffn_gain), f32(ffn_shift))
    layer_out = jnp.where(keep, normed_two, f32(row)).astype(B16)
    layer_out = deal(layer_out.reshape(blocks, block_len, D))

    grad_two = jnp.where(keep, f32(cot), 0.0)
    d_resid_two, ffn_gain_grad, ffn_shift_grad = norm_two_back(grad_two)
    d_ffn = d_resid_two.astype(B16)
    d_act = dot(d_ffn, contract, NT)
    d_pre = gelu_back(d_act)[0].astype(B16)
    d_normed = d_resid_two + dot(d_pre, expand, NT)
    d_resid_one, attn_gain_grad, attn_shift_grad = norm_one_back(d_normed)
    d_attn = d_resid_one.astype(B16)
    d_attended = dot(d_attn, mixing, NT).astype(B16)
    d_proj = jnp.concatenate(attend_back(qkv, probs, d_attended), axis=1)
    d_tokens = d_resid_one + dot(d_proj, projection, NT)
    tokens_grad = jnp.where(keep, d_tokens, f32(cot)).astype(B16)
    tokens_grad = deal(tokens_grad.reshape(blocks, block_len, D)).astype(F32)

    total = lambda a: jnp.sum(f32(a), axis=0)
    small = jnp.concatenate([total(d_proj[:, :D]), total(d_proj[:, 2 * D:]), total(d_attn), attn_gain_grad, attn_shift_grad,
        total(d_pre), total(d_ffn), ffn_gain_grad, ffn_shift_grad, jnp.zeros((4 * D,), F32)]).reshape(16, D)
    g, small = sum_grads(activated, d_ffn, normed_low, d_pre, attended, d_attn, row, d_proj, small)
    groups = lax.axis_size("dp") // 8
    if groups > 1:
        index = [[i + 8 * j for j in range(groups)] for i in range(8)]
        g, small = lax.psum((g, small), "dp", axis_index_groups=index)
    g = f32(g)
    contract_grad = g[:8].reshape(8 * CR, D)
    expand_grad = g[8:16].reshape(2, 4, CR, CC).transpose(0, 2, 1, 3).reshape(D, 4 * CC)
    mixing_grad = g[16:18].reshape(D, D)
    projection_grad = g[18:].reshape(2, 3, CR, CC).transpose(0, 2, 1, 3).reshape(D, 3 * D)
    return (layer_out, tokens_grad, projection_grad, small[:2], mixing_grad, small[2], small[3], small[4], expand_grad,
            small[5:9].reshape(-1), contract_grad, small[9], small[10], small[11])


def solution(mesh):
    data = P("dp", "blk", None)
    in_specs = (data, P("dp"), P("dp", "blk"), P("dp")) + (P(),) * 12 + (data,)
    out_specs = (data, data) + (P(),) * 12
    return jax.shard_map(local, mesh=mesh, in_specs=in_specs, out_specs=out_specs, check_vma=False)
```

time: 924 us -> 397 us (0.43)
  waiting for transfers between devices: 557 us -> 11.2 us
  Pallas kernels: 0 us -> 154 us
  blocking collectives: 59.2 us -> 0 us
  matrix products: 97.1 us -> 47.5 us
  other arithmetic: 44.5 us -> 20.6 us
  starting transfers between devices: 0.21 us -> 22.4 us
  local copies, waits for them, and re-layouts: 145 us -> 133 us
  between operations: 14.7 us -> 2.86 us
    psum x1 -> x0, waiting for transfers between devices: 372 us -> none  [local(): summed = lax.psum(attn_group + ffn_group, ('dp', 'blk'))]
    pallas_call x0 -> x3, Pallas kernels: none -> 154 us  [the longest x1 128 us: sum_grads(): pl.pallas_call(grads_kernel, out_shape=[jax.ShapeDtypeStruct((N, CR, CC),...]
    all_gather x2 -> x0, waiting for transfers between devices: 94.3 us -> none  [the longest x1 63.8 us: local(): lax.all_gather(values_own, 'blk', axis=1, tiled=True)]
    unnamed x7 -> x0, waiting for transfers between devices: 90.9 us -> none
    dot_general x40 -> x8, matrix products: 97.1 us -> 47.5 us  [dot(): return lax.dot_general(a, b, dims, preferred_element_type=F32)]
    psum x1 -> x0, blocking collectives: 43.9 us -> none  [local(): summed = lax.psum(attn_group + ffn_group, ('dp', 'blk'))]
    dynamic_slice x36 -> x7, local copies, waits for them, and re-layouts: 42.3 us -> 11.1 us  [the longest x5 8.63 us: deal(): piece = lax.dynamic_index_in_dim(blocks, z ^ m, 0)]
    slice x2 -> x6, local copies, waits for them, and re-layouts: 0.98 us -> 24.8 us  [the longest x1 12.7 us: local(): contract_grad = g[:8].reshape(8 * CR, D)]
  transfers between devices with their start and end apart: 5 -> 15, of which waited for: 5 -> 2; matrix products, arithmetic and copies ran while one was open for 7% -> 31% of each run, Pallas kernels for 0% -> 3%
where the time goes in v1:
time: 397 us; the launch traced here: 391 us
  Pallas kernels  154 us (39%)
  local copies, waits for them, and re-layouts  133 us (34%)
  matrix products  47.5 us (12%)
  starting transfers between devices  22.4 us (6%)
  other arithmetic  20.6 us (5%)
  waiting for transfers between devices  11.2 us (3%)
    pallas_call x1, Pallas kernels, sum_grads(): pl.pallas_call(grads_kernel, out_shape=[jax.ShapeDtypeStruct((N, CR, CC),...  128 us
    dot_general x8, matrix products, dot(): return lax.dot_general(a, b, dims, preferred_element_type=F32)  47.5 us
    unnamed x62, local copies, waits for them, and re-layouts  41.1 us
    ppermute x15, starting transfers between devices, deal(): piece = lax.ppermute(piece, 'blk', [(i, i ^ m) for i in range(n)])  22.4 us
    dynamic_update_slice x16, local copies, waits for them, and re-layouts, deal(): lax.dynamic_update_slice(out, piece, (z ^ m,) + (0,) * (blocks.ndim - 1))  20.7 us
    reshape x1, local copies, waits for them, and re-layouts, local(): g[18:].reshape(2, 3, CR, CC).transpose(0, 2, 1, 3).reshape(D, 3 * D)  13.8 us
    transpose x1, local copies, waits for them, and re-layouts, local(): g[8:16].reshape(2, 4, CR, CC).transpose(0, 2, 1, 3).reshape(D, 4 * CC)  13.4 us
    pallas_call x1, Pallas kernels, attend_back(): pl.pallas_call(bwd_kernel, grid=(G,), in_specs=[col(0), col(G), col(2 * G...  13.2 us
  transfers between devices with their start and end apart: 15, of which 2 were waited for; matrix products, arithmetic and copies ran while one was open for 31% of the time, Pallas kernels for 3%

profile of v1, /device:TPU:0, one launch (start us, length us, event | category | flops | bytes accessed | tf_op | source)
XLA Modules:
  0.0 391.1 jit_solution(5789404531654924497)
XLA Ops:
  2.2 5.0 %collective-permute-start.5 = (s32[1,1,128]{2,1,0:T(1,128)}, s32[1,1,128]{2,1,0:T(1,128)}, u32[]{:S(2)}, u32[]{:S(2)}) collective-permute-start(s32[1,1,128]{2,1,0:T(1,128)} %get-tuple-element.86), channel_id=1, source_target_pairs={{0,3},{1,2},{2,1},{3,0},{4,7},{5,6},{6,5},{7,4},{8,11},{9,10},{10,... | collective-permute-start | bytes 1544 | tf_op jit(solution)/shard_map/ppermute | solution.py:356
  10.8 3.8 collective-permute-start.2
  33.9 3.8 collective-permute-start.11
  43.5 9.3 %collective-permute-done.1 = bf16[1,128,768]{2,1,0:T(8,128)(2,1)} collective-permute-done((bf16[1,128,768]{2,1,0:T(8,128)(2,1)}, bf16[1,128,768]{2,1,0:T(8,128)(2,1)}, u32[]{:S(2)}, u32[]{:S(2)}) %collective-permute-start.1) | collective-permute-done | bytes 196640 | tf_op jit(solution)/shard_map/ppermute | solution.py:356
  56.0 3.1 fusion.6.q.k.v
  59.2 12.4 %attend.1 = (bf16[512,768]{1,0:T(8,128)(2,1)S(1)}, bf16[12,512,512]{2,1,0:T(8,128)(2,1)}) custom-call(bf16[512,2304]{1,0:T(8,128)(2,1)S(1)} %fusion.6.q.k.v, bf16[512,2304]{1,0:T(8,128)(2,1)S(1)} %fusion.6.q.k.v, bf16[512,2304]{1,0:T(8,128)(2,1)S(1)} %fusion.6.q.k.v, f32[512,512]{1,0:T(8,128)S(1)} %and_select_fusion.bias), custom_call_target="tpu_custom_call" | custom-call | flops 3221225472 | bytes 20971520 | tf_op jit(solution)/shard_map/attend/pallas_call | solution.py:38
  74.7 18.3 %multiply_convert_fusion = (bf16[512,3072]{1,0:T(8,128)(2,1)S(1)}, f32[512,3072]{1,0:T(8,128)}, f32[512,3072]{1,0:T(8,128)}) fusion(f32[3072]{0:T(1024)S(1)} %copy-done.16, bf16[512,768]{1,0:T(8,128)(2,1)S(1)} %fusion.16.low, bf16[768,3072]{1,0:T(8,128)(2,1)S(1)} %bitcast.85), kind=kOutput, calls=%fused_computation.4 | convolution fusion | flops 2519728128 | bytes 21245952 | tf_op jit(solution)/shard_map/dot_general | solution.py:21
  93.1 2.8 fusion.29
  103.4 3.2 fusion.25
  106.8 8.2 %convert_reduce_fusion = (f32[3072]{0:T(1024)S(1)}, bf16[512,3072]{1,0:T(8,128)(2,1)S(1)}) fusion(f32[512,3072]{1,0:T(8,128)} %get-tuple-element.66, f32[512,3072]{1,0:T(8,128)} %get-tuple-element.92, f32[3072]{0:T(1024)S(1)} %copy-done.16, bf16[512,768]{1,0:T(8,128)(2,1)S(1)} %get-tuple-element.56.d_ffn, bf16[3072,768]{1,0:T(8,128)(2,1)S(1)} %bitcast.83), kind=kOutput, calls=%fused_computation.2 | convolution fusion | flops 2442654720 | bytes 21258240 | tf_op jit(solution)/shard_map/dot_general | solution.py:21
  115.0 6.6 %multiply_reduce_fusion = (f32[768]{0:T(1024)S(1)}, f32[512]{0:T(512)S(1)}, f32[768]{0:T(1024)S(1)}, f32[512,768]{1,0:T(8,128)S(1)}) fusion(f32[512,768]{1,0:T(8,128)S(1)} %get-tuple-element.91, f32[512]{0:T(512)S(1)} %fusion.18, f32[512]{0:T(512)S(1)} %broadcast_multiply_fusion.1, f32[768]{0:T(1024)S(1)} %convert_element_type.102, ...), kind=kOutput, calls=%fused_computation.37 | convolution fusion | flops 2419849216 | bytes 12600320 | tf_op jit(solution)/shard_map/dot_general | solution.py:21
  123.6 13.2 %attend_back.1 = (bf16[512,768]{1,0:T(8,128)(2,1)S(1)}, bf16[512,768]{1,0:T(8,128)(2,1)S(1)}, bf16[512,768]{1,0:T(8,128)(2,1)S(1)}) custom-call(bf16[512,2304]{1,0:T(8,128)(2,1)S(1)} %fusion.6.q.k.v, bf16[512,2304]{1,0:T(8,128)(2,1)S(1)} %fusion.6.q.k.v, bf16[512,2304]{1,0:T(8,128)(2,1)S(1)} %fusion.6.q.k.v, bf16[12,512,512]{2,1,0:T(8,128)(2,1)} %get-tuple-element.22.probs, ...), custom_call_target="tpu_custom_call" | custom-call | flops 6442450944 | bytes 20971520 | tf_op jit(solution)/shard_map/attend_back/pallas_call | solution.py:65
  156.0 5.3 %fusion.15 = bf16[512,768]{1,0:T(8,128)(2,1)} fusion(bf16[4,128,768]{2,1,0:T(8,128)(2,1)} %constant_dynamic-update-slice_fusion.6, f32[512,768]{1,0:T(8,128)} %copy-done.4, bf16[512,2304]{1,0:T(8,128)(2,1)} %constant_dynamic-update-slice_fusion.d_proj, bf16[768,2304]{1,0:T(8,128)(2,1)S(1)} %copy-done, f32[512]{0:T(512)S(1)} %negate_multiply_fusion.1, pred[]{:T(512)} %bitcast), kind=kOutput, calls=%fused_computation.35 | convolution fusion | flops 1813905408 | bytes 9046017 | tf_op jit(solution)/shard_map/dot_general | solution.py:21
  161.3 128.1 %grads.1 = (bf16[24,384,768]{2,1,0:T(8,128)(2,1)}, f32[16,768]{1,0:T(8,128)}) custom-call(bf16[512,3072]{1,0:T(8,128)(2,1)} %copy-done.8, bf16[512,768]{1,0:T(8,128)(2,1)} %copy-done.6, bf16[512,768]{1,0:T(8,128)(2,1)} %copy-done.5, bf16[512,3072]{1,0:T(8,128)(2,1)} %copy-done.9, bf16[512,768]{1,0:T(8,128)(2,1)} %copy-done.2, bf16[512,768]{1,0:T(8,128)(2,1)} %copy-done.7, ...), custom_call_target="tpu_custom_call" | custom-call | tf_op jit(solution)/shard_map/grads/pallas_call | solution.py:332
  291.5 2.8 slice.57
  294.4 5.6 %slice.56 = f32[6,384,768]{2,1,0:T(8,128)} slice(bf16[24,384,768]{2,1,0:T(8,128)(2,1)} %get-tuple-element.26), slice={[18:24], [0:384], [0:768]} | slice | bytes 14155776 | tf_op jit(solution)/shard_map/slice | solution.py:425
  300.0 12.7 %fusion.27 = (f32[8,384,768]{2,1,0:T(8,128)}, f32[8,384,768]{2,1,0:T(8,128)}) fusion(bf16[24,384,768]{2,1,0:T(8,128)(2,1)} %get-tuple-element.26), kind=kLoop, calls=%fused_computation.127 | loop fusion | bytes 37748736 | tf_op jit(solution)/shard_map/slice | solution.py:422
  323.3 13.8 %copy.37 = f32[2,3,384,768]{2,0,3,1:T(2,128)} copy(f32[2,3,384,768]{3,2,1,0:T(8,128)} %bitcast.74) | data formatting | bytes 14155776 | tf_op jit(solution)/shard_map/reshape | solution.py:425
  337.1 6.4 %copy.40 = f32[288,8,2,384]{3,1,2,0:T(8,128)} copy(f32[288,8,2,384]{3,2,1,0:T(2,128)} %bitcast.75) | data formatting | bytes 14155776
  343.5 8.0 %copy.39 = f32[768,2304]{1,0:T(8,128)} copy(f32[768,2304]{0,1:T(8,128)} %bitcast.76) | data formatting | bytes 14155776
  351.4 13.4 %copy.38 = f32[2,384,4,768]{3,2,1,0:T(4,128)} copy(f32[2,384,4,768]{3,1,2,0:T(8,128)} %bitcast.73) | data formatting | bytes 18874368 | tf_op jit(solution)/shard_map/transpose | solution.py:423
  364.9 9.6 %copy.41 = f32[96,8,4,768]{3,1,2,0:T(8,128)} copy(f32[96,8,4,768]{3,2,1,0:T(4,128)} %bitcast.72) | data formatting | bytes 18874368
  376.1 2.7 collective-permute-start.14
  384.5 2.4 convert_element_type.118
  (154 shorter events, 87.6 us)
Async XLA Ops:
  0.6 55.4 %copy-start = (bf16[768,2304]{1,0:T(8,128)(2,1)S(1)}, bf16[768,2304]{1,0:T(8,128)(2,1)}, u32[]{:S(2)}) copy-start(bf16[768,2304]{1,0:T(8,128)(2,1)} %param.21) | copy-start | bytes 10616836
  2.2 36.8 %collective-permute-start.5 = (s32[1,1,128]{2,1,0:T(1,128)}, s32[1,1,128]{2,1,0:T(1,128)}, u32[]{:S(2)}, u32[]{:S(2)}) collective-permute-start(s32[1,1,128]{2,1,0:T(1,128)} %get-tuple-element.86), channel_id=1, source_target_pairs={{0,3},{1,2},{2,1},{3,0},{4,7},{5,6},{6,5},{7,4},{8,11},{9,10},{10,... | collective-permute-start | bytes 1544 | tf_op jit(solution)/shard_map/ppermute | solution.py:356
  7.2 24.8 %collective-permute-start.3 = (s32[1,1,128]{2,1,0:T(1,128)}, s32[1,1,128]{2,1,0:T(1,128)}, u32[]{:S(2)}, u32[]{:S(2)}) collective-permute-start(s32[1,1,128]{2,1,0:T(1,128)} %get-tuple-element.87), channel_id=1, source_target_pairs={{0,1},{1,0},{2,3},{3,2},{4,5},{5,4},{6,7},{7,6},{8,9},{9,8},{10,11... | collective-permute-start | bytes 1544 | tf_op jit(solution)/shard_map/ppermute | solution.py:356
  7.2 26.7 %collective-permute-start.4 = (s32[1,1,128]{2,1,0:T(1,128)}, s32[1,1,128]{2,1,0:T(1,128)}, u32[]{:S(2)}, u32[]{:S(2)}) collective-permute-start(s32[1,1,128]{2,1,0:T(1,128)} %get-tuple-element.89), channel_id=1, source_target_pairs={{0,2},{1,3},{2,0},{3,1},{4,6},{5,7},{6,4},{7,5},{8,10},{9,11},{10,... | collective-permute-start | bytes 1544 | tf_op jit(solution)/shard_map/ppermute | solution.py:356
  10.8 43.6 %collective-permute-start.2 = (bf16[1,128,768]{2,1,0:T(8,128)(2,1)}, bf16[1,128,768]{2,1,0:T(8,128)(2,1)}, u32[]{:S(2)}, u32[]{:S(2)}) collective-permute-start(bf16[1,128,768]{2,1,0:T(8,128)(2,1)} %get-tuple-element.82), channel_id=1, source_target_pairs={{0,3},{1,2},{2,1},{3,0},{4,7},{5,6},{6,5},{7,4},{8,11},{9,10},{10,... | collective-permute-start | bytes 589832 | tf_op jit(solution)/shard_map/ppermute | solution.py:356
  14.7 26.5 %collective-permute-start = (bf16[1,128,768]{2,1,0:T(8,128)(2,1)}, bf16[1,128,768]{2,1,0:T(8,128)(2,1)}, u32[]{:S(2)}, u32[]{:S(2)}) collective-permute-start(bf16[1,128,768]{2,1,0:T(8,128)(2,1)} %get-tuple-element.83), channel_id=1, source_target_pairs={{0,1},{1,0},{2,3},{3,2},{4,5},{5,4},{6,7},{7,6},{8,9},{9,8},{10,11... | collective-permute-start | bytes 589832 | tf_op jit(solution)/shard_map/ppermute | solution.py:356
  32.0 20.8 %collective-permute-start.1 = (bf16[1,128,768]{2,1,0:T(8,128)(2,1)}, bf16[1,128,768]{2,1,0:T(8,128)(2,1)}, u32[]{:S(2)}, u32[]{:S(2)}) collective-permute-start(bf16[1,128,768]{2,1,0:T(8,128)(2,1)} %get-tuple-element.85), channel_id=1, source_target_pairs={{0,2},{1,3},{2,0},{3,1},{4,6},{5,7},{6,4},{7,5},{8,10},{9,11},{10,... | collective-permute-start | bytes 589832 | tf_op jit(solution)/shard_map/ppermute | solution.py:356
  33.9 64.7 %collective-permute-start.11 = (bf16[1,128,768]{2,1,0:T(8,128)(2,1)}, bf16[1,128,768]{2,1,0:T(8,128)(2,1)}, u32[]{:S(2)}, u32[]{:S(2)}) collective-permute-start(bf16[1,128,768]{2,1,0:T(8,128)(2,1)} %get-tuple-element.74), channel_id=1, source_target_pairs={{0,3},{1,2},{2,1},{3,0},{4,7},{5,6},{6,5},{7,4},{8,11},{9,10},{10,... | collective-permute-start | bytes 589832 | tf_op jit(solution)/shard_map/ppermute | solution.py:356
  39.0 57.0 %collective-permute-start.9 = (bf16[1,128,768]{2,1,0:T(8,128)(2,1)}, bf16[1,128,768]{2,1,0:T(8,128)(2,1)}, u32[]{:S(2)}, u32[]{:S(2)}) collective-permute-start(bf16[1,128,768]{2,1,0:T(8,128)(2,1)} %get-tuple-element.75), channel_id=1, source_target_pairs={{0,1},{1,0},{2,3},{3,2},{4,5},{5,4},{6,7},{7,6},{8,9},{9,8},{10,11... | collective-permute-start | bytes 589832 | tf_op jit(solution)/shard_map/ppermute | solution.py:356
  41.2 56.7 %collective-permute-start.10 = (bf16[1,128,768]{2,1,0:T(8,128)(2,1)}, bf16[1,128,768]{2,1,0:T(8,128)(2,1)S(1)}, u32[]{:S(2)}, u32[]{:S(2)}) collective-permute-start(bf16[1,128,768]{2,1,0:T(8,128)(2,1)} %get-tuple-element.77), channel_id=1, source_target_pairs={{0,2},{1,3},{2,0},{3,1},{4,6},{5,7},{6,4},{7,5},{8,10},{9,11},{10,... | collective-permute-start | bytes 589832 | tf_op jit(solution)/shard_map/ppermute | solution.py:356
  59.2 12.4 %copy-start.18 = (f32[768]{0:T(1024)S(1)}, f32[768]{0:T(1024)}, u32[]{:S(2)}) copy-start(f32[768]{0:T(1024)} %convert_element_type.101) | copy-start | bytes 9220
  59.2 12.4 %copy-start.19 = (bf16[768,768]{1,0:T(8,128)(2,1)S(1)}, bf16[768,768]{1,0:T(8,128)(2,1)}, u32[]{:S(2)}) copy-start(bf16[768,768]{1,0:T(8,128)(2,1)} %param.23) | copy-start | bytes 3538948
  74.3 18.8 %slice-start = ((s8[4718592]{0:T(1024)(128)(4,1)}), s8[4194304]{0:T(1024)(128)(4,1)S(1)}, s32[]{:S(2)}) async-start(s8[4718592]{0:T(1024)(128)(4,1)} %bitcast.82), calls=%async_computation | async-start | bytes 8388608
  74.7 18.4 %copy-start.5 = (bf16[512,768]{1,0:T(8,128)(2,1)}, bf16[512,768]{1,0:T(8,128)(2,1)S(1)}, u32[]{:S(2)}) copy-start(bf16[512,768]{1,0:T(8,128)(2,1)S(1)} %fusion.16.low) | copy-start | bytes 2359300
  74.7 18.4 %copy-start.17 = (f32[768]{0:T(1024)S(1)}, f32[768]{0:T(1024)}, u32[]{:S(2)}) copy-start(f32[768]{0:T(1024)} %convert_element_type.107) | copy-start | bytes 9220
  74.7 18.4 %slice-start.1 = ((s8[4718592]{0:T(1024)(128)(4,1)}), s8[524288]{0:T(1024)(128)(4,1)S(1)}, s32[]{:S(2)}) async-start(s8[4718592]{0:T(1024)(128)(4,1)} %bitcast.82), calls=%async_computation.1 | async-start | bytes 1048576
  315.7 60.4 %collective-permute-start.12 = (bf16[1,128,768]{2,1,0:T(8,128)(2,1)}, bf16[1,128,768]{2,1,0:T(8,128)(2,1)}, u32[]{:S(2)}, u32[]{:S(2)}) collective-permute-start(bf16[1,128,768]{2,1,0:T(8,128)(2,1)} %get-tuple-element.72), channel_id=1, source_target_pairs={{0,1},{1,0},{2,3},{3,2},{4,5},{5,4},{6,7},{7,6},{8,9},{9,8},{10,11... | collective-permute-start | bytes 589832 | tf_op jit(solution)/shard_map/ppermute | solution.py:356
  317.5 71.3 %collective-permute-start.8 = (bf16[1,128,768]{2,1,0:T(8,128)(2,1)}, bf16[1,128,768]{2,1,0:T(8,128)(2,1)}, u32[]{:S(2)}, u32[]{:S(2)}) collective-permute-start(bf16[1,128,768]{2,1,0:T(8,128)(2,1)} %get-tuple-element.78), channel_id=1, source_target_pairs={{0,3},{1,2},{2,1},{3,0},{4,7},{5,6},{6,5},{7,4},{8,11},{9,10},{10,... | collective-permute-start | bytes 589832 | tf_op jit(solution)/shard_map/ppermute | solution.py:356
  318.6 69.2 %collective-permute-start.7 = (bf16[1,128,768]{2,1,0:T(8,128)(2,1)}, bf16[1,128,768]{2,1,0:T(8,128)(2,1)}, u32[]{:S(2)}, u32[]{:S(2)}) collective-permute-start(bf16[1,128,768]{2,1,0:T(8,128)(2,1)} %get-tuple-element.79), channel_id=1, source_target_pairs={{0,2},{1,3},{2,0},{3,1},{4,6},{5,7},{6,4},{7,5},{8,10},{9,11},{10,... | collective-permute-start | bytes 589832 | tf_op jit(solution)/shard_map/ppermute | solution.py:356
  321.0 65.9 %collective-permute-start.6 = (bf16[1,128,768]{2,1,0:T(8,128)(2,1)}, bf16[1,128,768]{2,1,0:T(8,128)(2,1)}, u32[]{:S(2)}, u32[]{:S(2)}) collective-permute-start(bf16[1,128,768]{2,1,0:T(8,128)(2,1)} %get-tuple-element.80), channel_id=1, source_target_pairs={{0,1},{1,0},{2,3},{3,2},{4,5},{5,4},{6,7},{7,6},{8,9},{9,8},{10,11... | collective-permute-start | bytes 589832 | tf_op jit(solution)/shard_map/ppermute | solution.py:356
  321.9 58.5 %collective-permute-start.13 = (bf16[1,128,768]{2,1,0:T(8,128)(2,1)}, bf16[1,128,768]{2,1,0:T(8,128)(2,1)}, u32[]{:S(2)}, u32[]{:S(2)}) collective-permute-start(bf16[1,128,768]{2,1,0:T(8,128)(2,1)} %get-tuple-element.71), channel_id=1, source_target_pairs={{0,2},{1,3},{2,0},{3,1},{4,6},{5,7},{6,4},{7,5},{8,10},{9,11},{10,... | collective-permute-start | bytes 589832 | tf_op jit(solution)/shard_map/ppermute | solution.py:356
  364.9 11.2 %copy-start.14 = (bf16[1,128,768]{2,1,0:T(8,128)(2,1)S(1)}, bf16[1,128,768]{2,1,0:T(8,128)(2,1)}, u32[]{:S(2)}) copy-start(bf16[1,128,768]{2,1,0:T(8,128)(2,1)} %get-tuple-element.70) | copy-start | bytes 589828
  374.5 12.4 %copy-start.12 = (bf16[4,128,768]{2,1,0:T(8,128)(2,1)S(1)}, bf16[4,128,768]{2,1,0:T(8,128)(2,1)}, u32[]{:S(2)}) copy-start(bf16[4,128,768]{2,1,0:T(8,128)(2,1)} %copy-done.11) | copy-start | bytes 2359300
  376.1 7.7 %collective-permute-start.14 = (bf16[1,128,768]{2,1,0:T(8,128)(2,1)S(1)}, bf16[1,128,768]{2,1,0:T(8,128)(2,1)S(1)}, u32[]{:S(2)}, u32[]{:S(2)}) collective-permute-start(bf16[1,128,768]{2,1,0:T(8,128)(2,1)S(1)} %copy-done.14), channel_id=1, source_target_pairs={{0,3},{1,2},{2,1},{3,0},{4,7},{5,6},{6,5},{7,4},{8,11},{9,10},{10,... | collective-permute-start | bytes 589832 | tf_op jit(solution)/shard_map/ppermute | solution.py:356
  (15 other events, 46.9 us)

commit v2 on v1

--- a/solution.py
+++ b/solution.py
@@ -346,6 +346,30 @@
     )(act, d_ffn, low, d_pre, att, d_att, tok, d_proj, small)
 
 
+def widen_kernel(g, contract, expand, mixing, projection):
+    i = pl.program_id(0)
+    for ref, first, last in ((contract, 0, 8), (expand, 8, 16), (mixing, 16, 18), (projection, 18, 24)):
+        @pl.when((i >= first) & (i < last))
+        def _():
+            ref[...] = g[0].astype(F32)
+
+
+def widen(g):
+    def spec(first, count, across):
+        def place(i):
+            j = jnp.clip(i - first, 0, count - 1)
+            return (j // across, j % across)
+        return pl.BlockSpec((CR, CC), place)
+    shape = lambda r, c: jax.ShapeDtypeStruct((r, c), F32)
+    return pl.pallas_call(widen_kernel, grid=(N,),
+        in_specs=[pl.BlockSpec((1, CR, CC), lambda i: (i, 0, 0))],
+        out_specs=[spec(0, 8, 1), spec(8, 8, 4), spec(16, 2, 1), spec(18, 6, 3)],
+        out_shape=[shape(4 * D, D), shape(D, 4 * D), shape(D, D), shape(D, 3 * D)],
+        compiler_params=pltpu.CompilerParams(vmem_limit_bytes=40 * 2**20),
+        cost_estimate=pl.CostEstimate(flops=0, bytes_accessed=6 * N * CR * CC, transcendentals=0),
+        name="widen")(g)
+
+
 def deal(blocks):
     z = lax.axis_index("blk")
     n = blocks.shape[0]
@@ -418,11 +442,7 @@
     if groups > 1:
         index = [[i + 8 * j for j in range(groups)] for i in range(8)]
         g, small = lax.psum((g, small), "dp", axis_index_groups=index)
-    g = f32(g)
-    contract_grad = g[:8].reshape(8 * CR, D)
-    expand_grad = g[8:16].reshape(2, 4, CR, CC).transpose(0, 2, 1, 3).reshape(D, 4 * CC)
-    mixing_grad = g[16:18].reshape(D, D)
-    projection_grad = g[18:].reshape(2, 3, CR, CC).transpose(0, 2, 1, 3).reshape(D, 3 * D)
+    contract_grad, expand_grad, mixing_grad, projection_grad = widen(g)
     return (layer_out, tokens_grad, projection_grad, small[:2], mixing_grad, small[2], small[3], small[4], expand_grad,
             small[5:9].reshape(-1), contract_grad, small[9], small[10], small[11])
 

time: 397 us -> 341 us (0.86)
  local copies, waits for them, and re-layouts: 133 us -> 66.7 us
  Pallas kernels: 154 us -> 168 us
    slice x3 -> x0, local copies, waits for them, and re-layouts: 21.1 us -> none  [the longest x1 12.7 us: local(): contract_grad = g[:8].reshape(8 * CR, D)]
    unnamed x62 -> x63, local copies, waits for them, and re-layouts: 41.1 us -> 23 us
    pallas_call x0 -> x1, Pallas kernels: none -> 14.8 us  [widen(): pl.pallas_call(widen_kernel, grid=(N,), in_specs=[pl.BlockSpec((1, CR, CC...]
    reshape x1 -> x0, local copies, waits for them, and re-layouts: 13.8 us -> none  [local(): g[18:].reshape(2, 3, CR, CC).transpose(0, 2, 1, 3).reshape(D, 3 * D)]
    transpose x1 -> x0, local copies, waits for them, and re-layouts: 13.4 us -> none  [local(): g[8:16].reshape(2, 4, CR, CC).transpose(0, 2, 1, 3).reshape(D, 4 * CC)]
  transfers between devices with their start and end apart: 15 -> 15, of which waited for: 2 -> 2; matrix products, arithmetic and copies ran while one was open for 31% -> 21% of each run, Pallas kernels for 3% -> 8%
where the time goes in v2:
time: 341 us; the launch traced here: 339 us
  Pallas kernels  168 us (49%)
  local copies, waits for them, and re-layouts  66.7 us (20%)
  matrix products  46.9 us (14%)
  starting transfers between devices  22.3 us (7%)
  other arithmetic  20.6 us (6%)
  waiting for transfers between devices  11.2 us (3%)
    pallas_call x1, Pallas kernels, sum_grads(): pl.pallas_call(grads_kernel, out_shape=[jax.ShapeDtypeStruct((N, CR, CC),...  128 us
    dot_general x8, matrix products, dot(): return lax.dot_general(a, b, dims, preferred_element_type=F32)  46.9 us
    unnamed x63, local copies, waits for them, and re-layouts  23 us
    ppermute x15, starting transfers between devices, deal(): piece = lax.ppermute(piece, 'blk', [(i, i ^ m) for i in range(n)])  22.3 us
    dynamic_update_slice x16, local copies, waits for them, and re-layouts, deal(): lax.dynamic_update_slice(out, piece, (z ^ m,) + (0,) * (blocks.ndim - 1))  20.7 us
    pallas_call x1, Pallas kernels, widen(): pl.pallas_call(widen_kernel, grid=(N,), in_specs=[pl.BlockSpec((1, CR, CC...  14.8 us
    pallas_call x1, Pallas kernels, attend_back(): pl.pallas_call(bwd_kernel, grid=(G,), in_specs=[col(0), col(G), col(2 * G...  13.2 us
    pallas_call x1, Pallas kernels, attend(): pl.pallas_call(fwd_kernel, grid=(G,), in_specs=[col(0), col(G), col(2 * G...  12.4 us
  transfers between devices with their start and end apart: 15, of which 2 were waited for; matrix products, arithmetic and copies ran while one was open for 21% of the time, Pallas kernels for 8%

profile of v2, /device:TPU:0, one launch (start us, length us, event | category | flops | bytes accessed | tf_op | source)
XLA Modules:
  0.0 338.6 jit_solution(16499493128232757942)
XLA Ops:
  2.2 5.0 %collective-permute-start.5 = (s32[1,1,128]{2,1,0:T(1,128)}, s32[1,1,128]{2,1,0:T(1,128)}, u32[]{:S(2)}, u32[]{:S(2)}) collective-permute-start(s32[1,1,128]{2,1,0:T(1,128)} %get-tuple-element.78), channel_id=1, source_target_pairs={{0,3},{1,2},{2,1},{3,0},{4,7},{5,6},{6,5},{7,4},{8,11},{9,10},{10,... | collective-permute-start | bytes 1544 | tf_op jit(solution)/shard_map/ppermute | solution.py:380
  8.7 2.1 constant_dynamic-slice_fusion.12
  10.8 3.8 %collective-permute-start.2 = (bf16[1,128,768]{2,1,0:T(8,128)(2,1)}, bf16[1,128,768]{2,1,0:T(8,128)(2,1)}, u32[]{:S(2)}, u32[]{:S(2)}) collective-permute-start(bf16[1,128,768]{2,1,0:T(8,128)(2,1)} %get-tuple-element.74), channel_id=1, source_target_pairs={{0,3},{1,2},{2,1},{3,0},{4,7},{5,6},{6,5},{7,4},{8,11},{9,10},{10,... | collective-permute-start | bytes 589832 | tf_op jit(solution)/shard_map/ppermute | solution.py:380
  22.3 2.1 constant_dynamic-slice_fusion.1
  33.9 3.8 %collective-permute-start.11 = (bf16[1,128,768]{2,1,0:T(8,128)(2,1)}, bf16[1,128,768]{2,1,0:T(8,128)(2,1)}, u32[]{:S(2)}, u32[]{:S(2)}) collective-permute-start(bf16[1,128,768]{2,1,0:T(8,128)(2,1)} %get-tuple-element.66), channel_id=1, source_target_pairs={{0,3},{1,2},{2,1},{3,0},{4,7},{5,6},{6,5},{7,4},{8,11},{9,10},{10,... | collective-permute-start | bytes 589832 | tf_op jit(solution)/shard_map/ppermute | solution.py:380
  43.5 9.3 %collective-permute-done.1 = bf16[1,128,768]{2,1,0:T(8,128)(2,1)} collective-permute-done((bf16[1,128,768]{2,1,0:T(8,128)(2,1)}, bf16[1,128,768]{2,1,0:T(8,128)(2,1)}, u32[]{:S(2)}, u32[]{:S(2)}) %collective-permute-start.1) | collective-permute-done | bytes 196640 | tf_op jit(solution)/shard_map/ppermute | solution.py:380
  56.0 3.1 fusion.6.q.k.v
  59.2 12.4 %attend.1 = (bf16[512,768]{1,0:T(8,128)(2,1)S(1)}, bf16[12,512,512]{2,1,0:T(8,128)(2,1)}) custom-call(bf16[512,2304]{1,0:T(8,128)(2,1)S(1)} %fusion.6.q.k.v, bf16[512,2304]{1,0:T(8,128)(2,1)S(1)} %fusion.6.q.k.v, bf16[512,2304]{1,0:T(8,128)(2,1)S(1)} %fusion.6.q.k.v, f32[512,512]{1,0:T(8,128)S(1)} %and_select_fusion.bias), custom_call_target="tpu_custom_call" | custom-call | flops 3221225472 | bytes 20971520 | tf_op jit(solution)/shard_map/attend/pallas_call | solution.py:38
  71.7 2.3 fusion.27
  74.8 18.3 %multiply_convert_fusion = (bf16[512,3072]{1,0:T(8,128)(2,1)S(1)}, f32[512,3072]{1,0:T(8,128)}, f32[512,3072]{1,0:T(8,128)}) fusion(f32[3072]{0:T(1024)S(1)} %copy-done.18, bf16[512,768]{1,0:T(8,128)(2,1)S(1)} %fusion.16.low, bf16[768,3072]{1,0:T(8,128)(2,1)S(1)} %bitcast.62), kind=kOutput, calls=%fused_computation.4 | convolution fusion | flops 2519728128 | bytes 21245952 | tf_op jit(solution)/shard_map/dot_general | solution.py:21
  93.2 2.8 fusion.28
  103.5 3.2 fusion.25
  106.9 8.2 %convert_reduce_fusion = (f32[3072]{0:T(1024)S(1)}, bf16[512,3072]{1,0:T(8,128)(2,1)S(1)}) fusion(f32[512,3072]{1,0:T(8,128)} %get-tuple-element.60, f32[512,3072]{1,0:T(8,128)} %get-tuple-element.84, f32[3072]{0:T(1024)S(1)} %copy-done.18, bf16[512,768]{1,0:T(8,128)(2,1)S(1)} %get-tuple-element.50.d_ffn, bf16[3072,768]{1,0:T(8,128)(2,1)S(1)} %bitcast.60), kind=kOutput, calls=%fused_computation.2 | convolution fusion | flops 2442654720 | bytes 21258240 | tf_op jit(solution)/shard_map/dot_general | solution.py:21
  115.1 6.6 %multiply_reduce_fusion = (f32[768]{0:T(1024)S(1)}, f32[512]{0:T(512)S(1)}, f32[768]{0:T(1024)S(1)}, f32[512,768]{1,0:T(8,128)S(1)}) fusion(f32[512,768]{1,0:T(8,128)S(1)} %get-tuple-element.83, f32[512]{0:T(512)S(1)} %fusion.18, f32[512]{0:T(512)S(1)} %broadcast_multiply_fusion.1, f32[768]{0:T(1024)S(1)} %convert_element_type.99, ...), kind=kOutput, calls=%fused_computation.37 | convolution fusion | flops 2419849216 | bytes 12600320 | tf_op jit(solution)/shard_map/dot_general | solution.py:21
  124.3 13.2 %attend_back.1 = (bf16[512,768]{1,0:T(8,128)(2,1)S(1)}, bf16[512,768]{1,0:T(8,128)(2,1)S(1)}, bf16[512,768]{1,0:T(8,128)(2,1)S(1)}) custom-call(bf16[512,2304]{1,0:T(8,128)(2,1)S(1)} %fusion.6.q.k.v, bf16[512,2304]{1,0:T(8,128)(2,1)S(1)} %fusion.6.q.k.v, bf16[512,2304]{1,0:T(8,128)(2,1)S(1)} %fusion.6.q.k.v, bf16[12,512,512]{2,1,0:T(8,128)(2,1)} %get-tuple-element.26.probs, ...), custom_call_target="tpu_custom_call" | custom-call | flops 6442450944 | bytes 20971520 | tf_op jit(solution)/shard_map/attend_back/pallas_call | solution.py:65
  152.6 2.2 constant_dynamic-update-slice_fusion.1
  156.8 4.8 %fusion.15 = bf16[512,768]{1,0:T(8,128)(2,1)} fusion(bf16[4,128,768]{2,1,0:T(8,128)(2,1)} %constant_dynamic-update-slice_fusion.6, f32[512,768]{1,0:T(8,128)S(1)} %copy-done.6, bf16[512,2304]{1,0:T(8,128)(2,1)} %constant_dynamic-update-slice_fusion.d_proj, bf16[768,2304]{1,0:T(8,128)(2,1)S(1)} %copy-done, f32[512]{0:T(512)S(1)} %negate_multiply_fusion.1, ...), kind=kOutput, calls=%fused_computation.35 | convolution fusion | flops 1813905408 | bytes 9046017 | tf_op jit(solution)/shard_map/dot_general | solution.py:21
  161.6 128.1 %grads.1 = (bf16[24,384,768]{2,1,0:T(8,128)(2,1)}, f32[16,768]{1,0:T(8,128)}) custom-call(bf16[512,3072]{1,0:T(8,128)(2,1)} %copy-done.10, bf16[512,768]{1,0:T(8,128)(2,1)} %copy-done.8, bf16[512,768]{1,0:T(8,128)(2,1)} %copy-done.7, bf16[512,3072]{1,0:T(8,128)(2,1)} %copy-done.11, bf16[512,768]{1,0:T(8,128)(2,1)} %copy-done.3, bf16[512,768]{1,0:T(8,128)(2,1)} %copy-done.9, ...), custom_call_target="tpu_custom_call" | custom-call | tf_op jit(solution)/shard_map/grads/pallas_call | solution.py:332
  292.9 2.1 constant_dynamic-slice_fusion.4
  298.1 2.3 collective-permute-start.7
  302.7 5.0 %copy-done.1 = bf16[24,384,768]{2,1,0:T(8,128)(2,1)S(1)} copy-done((bf16[24,384,768]{2,1,0:T(8,128)(2,1)S(1)}, bf16[24,384,768]{2,1,0:T(8,128)(2,1)}, u32[]{:S(2)}) %copy-start.1) | copy-done | bytes 14155800
  307.8 14.8 %widen.1 = (f32[3072,768]{1,0:T(8,128)}, f32[768,3072]{1,0:T(8,128)}, f32[768,768]{1,0:T(8,128)}, f32[768,2304]{1,0:T(8,128)}) custom-call(bf16[24,384,768]{2,1,0:T(8,128)(2,1)S(1)} %copy-done.1), custom_call_target="tpu_custom_call" | custom-call | bytes 42467328 | tf_op jit(solution)/shard_map/widen/pallas_call | solution.py:364
  324.1 2.6 collective-permute-start.14
  332.5 2.4 convert_element_type.115
  (151 shorter events, 75.7 us)
Async XLA Ops:
  0.6 55.4 %copy-start = (bf16[768,2304]{1,0:T(8,128)(2,1)S(1)}, bf16[768,2304]{1,0:T(8,128)(2,1)}, u32[]{:S(2)}) copy-start(bf16[768,2304]{1,0:T(8,128)(2,1)} %param.21) | copy-start | bytes 10616836
  2.2 36.8 %collective-permute-start.5 = (s32[1,1,128]{2,1,0:T(1,128)}, s32[1,1,128]{2,1,0:T(1,128)}, u32[]{:S(2)}, u32[]{:S(2)}) collective-permute-start(s32[1,1,128]{2,1,0:T(1,128)} %get-tuple-element.78), channel_id=1, source_target_pairs={{0,3},{1,2},{2,1},{3,0},{4,7},{5,6},{6,5},{7,4},{8,11},{9,10},{10,... | collective-permute-start | bytes 1544 | tf_op jit(solution)/shard_map/ppermute | solution.py:380
  7.2 24.8 %collective-permute-start.3 = (s32[1,1,128]{2,1,0:T(1,128)}, s32[1,1,128]{2,1,0:T(1,128)}, u32[]{:S(2)}, u32[]{:S(2)}) collective-permute-start(s32[1,1,128]{2,1,0:T(1,128)} %get-tuple-element.79), channel_id=1, source_target_pairs={{0,1},{1,0},{2,3},{3,2},{4,5},{5,4},{6,7},{7,6},{8,9},{9,8},{10,11... | collective-permute-start | bytes 1544 | tf_op jit(solution)/shard_map/ppermute | solution.py:380
  7.2 26.7 %collective-permute-start.4 = (s32[1,1,128]{2,1,0:T(1,128)}, s32[1,1,128]{2,1,0:T(1,128)}, u32[]{:S(2)}, u32[]{:S(2)}) collective-permute-start(s32[1,1,128]{2,1,0:T(1,128)} %get-tuple-element.81), channel_id=1, source_target_pairs={{0,2},{1,3},{2,0},{3,1},{4,6},{5,7},{6,4},{7,5},{8,10},{9,11},{10,... | collective-permute-start | bytes 1544 | tf_op jit(solution)/shard_map/ppermute | solution.py:380
  10.8 43.6 %collective-permute-start.2 = (bf16[1,128,768]{2,1,0:T(8,128)(2,1)}, bf16[1,128,768]{2,1,0:T(8,128)(2,1)}, u32[]{:S(2)}, u32[]{:S(2)}) collective-permute-start(bf16[1,128,768]{2,1,0:T(8,128)(2,1)} %get-tuple-element.74), channel_id=1, source_target_pairs={{0,3},{1,2},{2,1},{3,0},{4,7},{5,6},{6,5},{7,4},{8,11},{9,10},{10,... | collective-permute-start | bytes 589832 | tf_op jit(solution)/shard_map/ppermute | solution.py:380
  14.7 26.5 %collective-permute-start = (bf16[1,128,768]{2,1,0:T(8,128)(2,1)}, bf16[1,128,768]{2,1,0:T(8,128)(2,1)}, u32[]{:S(2)}, u32[]{:S(2)}) collective-permute-start(bf16[1,128,768]{2,1,0:T(8,128)(2,1)} %get-tuple-element.75), channel_id=1, source_target_pairs={{0,1},{1,0},{2,3},{3,2},{4,5},{5,4},{6,7},{7,6},{8,9},{9,8},{10,11... | collective-permute-start | bytes 589832 | tf_op jit(solution)/shard_map/ppermute | solution.py:380
  32.0 20.8 %collective-permute-start.1 = (bf16[1,128,768]{2,1,0:T(8,128)(2,1)}, bf16[1,128,768]{2,1,0:T(8,128)(2,1)}, u32[]{:S(2)}, u32[]{:S(2)}) collective-permute-start(bf16[1,128,768]{2,1,0:T(8,128)(2,1)} %get-tuple-element.77), channel_id=1, source_target_pairs={{0,2},{1,3},{2,0},{3,1},{4,6},{5,7},{6,4},{7,5},{8,10},{9,11},{10,... | collective-permute-start | bytes 589832 | tf_op jit(solution)/shard_map/ppermute | solution.py:380
  33.9 64.8 %collective-permute-start.11 = (bf16[1,128,768]{2,1,0:T(8,128)(2,1)}, bf16[1,128,768]{2,1,0:T(8,128)(2,1)}, u32[]{:S(2)}, u32[]{:S(2)}) collective-permute-start(bf16[1,128,768]{2,1,0:T(8,128)(2,1)} %get-tuple-element.66), channel_id=1, source_target_pairs={{0,3},{1,2},{2,1},{3,0},{4,7},{5,6},{6,5},{7,4},{8,11},{9,10},{10,... | collective-permute-start | bytes 589832 | tf_op jit(solution)/shard_map/ppermute | solution.py:380
  39.0 57.1 %collective-permute-start.9 = (bf16[1,128,768]{2,1,0:T(8,128)(2,1)}, bf16[1,128,768]{2,1,0:T(8,128)(2,1)}, u32[]{:S(2)}, u32[]{:S(2)}) collective-permute-start(bf16[1,128,768]{2,1,0:T(8,128)(2,1)} %get-tuple-element.67), channel_id=1, source_target_pairs={{0,1},{1,0},{2,3},{3,2},{4,5},{5,4},{6,7},{7,6},{8,9},{9,8},{10,11... | collective-permute-start | bytes 589832 | tf_op jit(solution)/shard_map/ppermute | solution.py:380
  41.2 56.8 %collective-permute-start.10 = (bf16[1,128,768]{2,1,0:T(8,128)(2,1)}, bf16[1,128,768]{2,1,0:T(8,128)(2,1)S(1)}, u32[]{:S(2)}, u32[]{:S(2)}) collective-permute-start(bf16[1,128,768]{2,1,0:T(8,128)(2,1)} %get-tuple-element.69), channel_id=1, source_target_pairs={{0,2},{1,3},{2,0},{3,1},{4,6},{5,7},{6,4},{7,5},{8,10},{9,11},{10,... | collective-permute-start | bytes 589832 | tf_op jit(solution)/shard_map/ppermute | solution.py:380
  59.2 12.5 %copy-start.20 = (f32[768]{0:T(1024)S(1)}, f32[768]{0:T(1024)}, u32[]{:S(2)}) copy-start(f32[768]{0:T(1024)} %convert_element_type.98) | copy-start | bytes 9220
  59.2 12.4 %copy-start.21 = (bf16[768,768]{1,0:T(8,128)(2,1)S(1)}, bf16[768,768]{1,0:T(8,128)(2,1)}, u32[]{:S(2)}) copy-start(bf16[768,768]{1,0:T(8,128)(2,1)} %param.23) | copy-start | bytes 3538948
  74.3 18.8 %slice-start = ((s8[4718592]{0:T(1024)(128)(4,1)}), s8[4194304]{0:T(1024)(128)(4,1)S(1)}, s32[]{:S(2)}) async-start(s8[4718592]{0:T(1024)(128)(4,1)} %bitcast.59), calls=%async_computation | async-start | bytes 8388608
  74.8 18.3 %copy-start.7 = (bf16[512,768]{1,0:T(8,128)(2,1)}, bf16[512,768]{1,0:T(8,128)(2,1)S(1)}, u32[]{:S(2)}) copy-start(bf16[512,768]{1,0:T(8,128)(2,1)S(1)} %fusion.16.low) | copy-start | bytes 2359300
  74.8 18.3 %copy-start.19 = (f32[768]{0:T(1024)S(1)}, f32[768]{0:T(1024)}, u32[]{:S(2)}) copy-start(f32[768]{0:T(1024)} %convert_element_type.104) | copy-start | bytes 9220
  74.8 18.4 %slice-start.1 = ((s8[4718592]{0:T(1024)(128)(4,1)}), s8[524288]{0:T(1024)(128)(4,1)S(1)}, s32[]{:S(2)}) async-start(s8[4718592]{0:T(1024)(128)(4,1)} %bitcast.59), calls=%async_computation.1 | async-start | bytes 1048576
  295.0 29.1 %collective-permute-start.12 = (bf16[1,128,768]{2,1,0:T(8,128)(2,1)}, bf16[1,128,768]{2,1,0:T(8,128)(2,1)}, u32[]{:S(2)}, u32[]{:S(2)}) collective-permute-start(bf16[1,128,768]{2,1,0:T(8,128)(2,1)} %get-tuple-element.64), channel_id=1, source_target_pairs={{0,1},{1,0},{2,3},{3,2},{4,5},{5,4},{6,7},{7,6},{8,9},{9,8},{10,11... | collective-permute-start | bytes 589832 | tf_op jit(solution)/shard_map/ppermute | solution.py:380
  296.8 40.0 %collective-permute-start.8 = (bf16[1,128,768]{2,1,0:T(8,128)(2,1)}, bf16[1,128,768]{2,1,0:T(8,128)(2,1)}, u32[]{:S(2)}, u32[]{:S(2)}) collective-permute-start(bf16[1,128,768]{2,1,0:T(8,128)(2,1)} %get-tuple-element.70), channel_id=1, source_target_pairs={{0,3},{1,2},{2,1},{3,0},{4,7},{5,6},{6,5},{7,4},{8,11},{9,10},{10,... | collective-permute-start | bytes 589832 | tf_op jit(solution)/shard_map/ppermute | solution.py:380
  298.1 37.7 %collective-permute-start.7 = (bf16[1,128,768]{2,1,0:T(8,128)(2,1)}, bf16[1,128,768]{2,1,0:T(8,128)(2,1)}, u32[]{:S(2)}, u32[]{:S(2)}) collective-permute-start(bf16[1,128,768]{2,1,0:T(8,128)(2,1)} %get-tuple-element.71), channel_id=1, source_target_pairs={{0,2},{1,3},{2,0},{3,1},{4,6},{5,7},{6,4},{7,5},{8,10},{9,11},{10,... | collective-permute-start | bytes 589832 | tf_op jit(solution)/shard_map/ppermute | solution.py:380
  300.3 34.5 %collective-permute-start.6 = (bf16[1,128,768]{2,1,0:T(8,128)(2,1)}, bf16[1,128,768]{2,1,0:T(8,128)(2,1)}, u32[]{:S(2)}, u32[]{:S(2)}) collective-permute-start(bf16[1,128,768]{2,1,0:T(8,128)(2,1)} %get-tuple-element.72), channel_id=1, source_target_pairs={{0,1},{1,0},{2,3},{3,2},{4,5},{5,4},{6,7},{7,6},{8,9},{9,8},{10,11... | collective-permute-start | bytes 589832 | tf_op jit(solution)/shard_map/ppermute | solution.py:380
  301.2 27.1 %collective-permute-start.13 = (bf16[1,128,768]{2,1,0:T(8,128)(2,1)}, bf16[1,128,768]{2,1,0:T(8,128)(2,1)}, u32[]{:S(2)}, u32[]{:S(2)}) collective-permute-start(bf16[1,128,768]{2,1,0:T(8,128)(2,1)} %get-tuple-element.63), channel_id=1, source_target_pairs={{0,2},{1,3},{2,0},{3,1},{4,6},{5,7},{6,4},{7,5},{8,10},{9,11},{10,... | collective-permute-start | bytes 589832 | tf_op jit(solution)/shard_map/ppermute | solution.py:380
  307.8 16.3 %copy-start.16 = (bf16[1,128,768]{2,1,0:T(8,128)(2,1)S(1)}, bf16[1,128,768]{2,1,0:T(8,128)(2,1)}, u32[]{:S(2)}) copy-start(bf16[1,128,768]{2,1,0:T(8,128)(2,1)} %get-tuple-element.62) | copy-start | bytes 589828
  322.5 12.3 %copy-start.14 = (bf16[4,128,768]{2,1,0:T(8,128)(2,1)S(1)}, bf16[4,128,768]{2,1,0:T(8,128)(2,1)}, u32[]{:S(2)}) copy-start(bf16[4,128,768]{2,1,0:T(8,128)(2,1)} %copy-done.13) | copy-start | bytes 2359300
  324.1 7.7 %collective-permute-start.14 = (bf16[1,128,768]{2,1,0:T(8,128)(2,1)S(1)}, bf16[1,128,768]{2,1,0:T(8,128)(2,1)S(1)}, u32[]{:S(2)}, u32[]{:S(2)}) collective-permute-start(bf16[1,128,768]{2,1,0:T(8,128)(2,1)S(1)} %copy-done.16), channel_id=1, source_target_pairs={{0,3},{1,2},{2,1},{3,0},{4,7},{5,6},{6,5},{7,4},{8,11},{9,10},{10,... | collective-permute-start | bytes 589832 | tf_op jit(solution)/shard_map/ppermute | solution.py:380
  (17 other events, 55.6 us)

commit v3 on v2

v3 whole, which is shorter than its diff:
```python
import functools

import jax
import jax.numpy as jnp
from jax import lax
from jax.experimental import pallas as pl
from jax.experimental.pallas import tpu as pltpu
from jax.sharding import PartitionSpec as P

D = 768
FF = 3072
HEADS = 12
HEAD_DIM = 64
DOC_SHORT = 128
MESH = pl.DeviceIdType.MESH
EPS = 1e-05
NEG = -1e9
F32, B16 = jnp.float32, jnp.bfloat16
NN = (((1,), (0,)), ((), ()))
NT = (((1,), (1,)), ((), ()))
TN = (((0,), (0,)), ((), ()))

CR, CC = 384, 768
HR, HC = CR // 2, CC // 2
SR = HR // 4
N = 24
KINDS = 12
CORE, FIRST, ZA, ZB, ZC, LAST, GR, GL, GF, GE, AGF, AGC = range(KINDS)
OFF = [0, 1, 4, 6, 8, 10, 12, 14, 16, 18, 21, 22]
VECS = 16


def dot(a, b, dims=NN):
    return lax.dot_general(a, b, dims, preferred_element_type=F32)


def rows(start, n):
    return pl.ds(pl.multiple_of(start, 16), n)


def cols(start, n):
    return pl.ds(pl.multiple_of(start, 128), n)


def normal_parts(v):
    t = 1.0 / (1.0 + (0.3275911 * 0.5 ** 0.5) * jnp.abs(v))
    ex = jnp.exp(-0.5 * (v * v))
    poly = t * (0.127414796 + t * (-0.142248368 + t * (0.7107068705 + t * (-0.7265760135 + t * 0.5307027145))))
    tail = poly * ex
    below = jnp.where(v < 0, tail, 1.0 - tail)
    return v * below, below + v * (ex * 0.3989422804014327)


def mean(a):
    return jnp.sum(a, axis=1, keepdims=True) * (1.0 / D)


def layer_kernel(kinds, keeps, vecs, ebias, live, tokens, cot_in, w_proj, w_mix, w_exp, w_con,
                 g_out, small_out, out_l, out_t,
                 wproj, wmix, wexp, wcon, row, cot, livebuf, qkv, att, probs, low, act, gp, xhat, dres, d_ffn, d_attn, d_att,
                 send, rstd, bias,
                 part, r0, r1, za, zb, zc, fin, sm, smr,
                 ssem, rsem, lsem, smss, smrs, wsem, dsend, drecv, dloc):
    dp, z = lax.axis_index("dp"), lax.axis_index("blk")
    T = row.shape[0]
    BL = T // 4
    c, x, y = dp % 2, (dp // 2) % 2, (dp // 4) % 2
    d_core = (dp + 1 - 2 * c, z)
    d_x = (dp + 2 - 4 * x, z)
    d_y = (dp + 4 - 8 * y, z)
    right, left = (dp, jnp.minimum(z + 1, 3)), (dp, jnp.maximum(z - 1, 0))
    is0, is1, is2, is3 = z == 0, z == 1, z == 2, z == 3
    end, mid = (z == 0) | (z == 3), (z == 1) | (z == 2)
    others = (z, z + 1 - 2 * (z % 2), z + 2 - 4 * (z // 2), 3 - z)

    loads = [pltpu.make_async_copy(a, b, wsem.at[i]) for i, (a, b) in
             enumerate(((w_proj, wproj), (w_mix, wmix), (w_exp, wexp), (w_con, wcon)))]

    barrier = pltpu.get_barrier_semaphore()
    for d in (d_core, d_x, d_y) + tuple((dp, others[m]) for m in (1, 2, 3)):
        pl.semaphore_signal(barrier, inc=1, device_id=d, device_id_type=MESH)
    pl.semaphore_wait(barrier, 6)

    TOK, LIVE, COT, OUTL, OUTT = range(5)

    def deal(kind, m, arriving=False):
        there = others[m]
        src, dst = {
            TOK: lambda: (tokens.at[there], row.at[rows((there if arriving else z) * BL, BL)]),
            LIVE: lambda: (live.at[there], livebuf.at[there if arriving else z]),
            COT: lambda: (cot_in.at[there], cot.at[rows((there if arriving else z) * BL, BL)]),
            OUTL: lambda: (send.at[rows(there * BL, BL)], out_l.at[there if arriving else z]),
            OUTT: lambda: (send.at[rows(there * BL, BL)], out_t.at[there if arriving else z]),
        }[kind]()
        if m == 0:
            return pltpu.make_async_copy(src, dst, dloc.at[kind])
        return pltpu.make_async_remote_copy(src_ref=src, dst_ref=dst, send_sem=dsend.at[kind, m], recv_sem=drecv.at[kind, m],
                                            device_id=(dp, there), device_id_type=MESH)

    def finish(kind):
        for m in (1, 2, 3):
            deal(kind, m).wait_send()

    for m in (3, 2, 1, 0):
        deal(LIVE, m).start()
        deal(TOK, m).start()
    for load in loads:
        load.start()

    def project(m):
        (deal(TOK, 0).wait if m == 0 else deal(TOK, m, True).wait_recv)()
        r = rows(others[m] * BL, BL)
        for j in range(3):
            s = slice(j * D, (j + 1) * D)
            part_j = dot(row[r], wproj[:, s]) + vecs[j:j + 1]
            if j == 0:
                part_j = part_j.astype(B16).astype(F32) * HEAD_DIM ** -0.5
            qkv[r, s] = part_j.astype(B16)

    loads[0].wait()
    for m in (0, 1, 2, 3):
        project(m)
    for m in (3, 2, 1, 0):
        deal(COT, m).start()

    deal(LIVE, 0).wait()
    for m in (1, 2, 3):
        deal(LIVE, m, True).wait_recv()
    count = jnp.sum(jnp.sum(livebuf[...], axis=0), axis=1, keepdims=True)
    short = (1 - kinds[z]).astype(F32) * NEG
    for b in range(4):
        key = lax.broadcasted_iota(jnp.int32, (BL, T), 0) + b * BL
        query = lax.broadcasted_iota(jnp.int32, (BL, T), 1)
        shift = DOC_SHORT.bit_length() - 1
        apart = jnp.where((key >> shift) == (query >> shift), 0.0, short)
        bias[b * BL:(b + 1) * BL] = jnp.where(key < count, apart, NEG)

    def attend(i, _):
        s = cols(i * 2 * HEAD_DIM, 2 * HEAD_DIM)
        q2, k2, v2 = (qkv[:, cols(j * D + i * 2 * HEAD_DIM, 2 * HEAD_DIM)] for j in range(3))
        outs = []
        for h in range(2):
            hs = slice(h * HEAD_DIM, (h + 1) * HEAD_DIM)
            scores = dot(k2[:, hs], q2[:, hs], NT) + bias[...]
            e = jnp.exp(scores - jnp.max(scores, axis=0, keepdims=True))
            p = (e * (1.0 / jnp.sum(e, axis=0, keepdims=True))).astype(B16)
            probs[2 * i + h] = p
            outs.append(dot(v2[:, hs], p, TN))
        att[:, s] = jnp.concatenate(outs, axis=0).T.astype(B16)
        return 0
    lax.fori_loop(0, HEADS // 2, attend, 0)

    loads[1].wait()
    RB = 256

    def norm_one(i, _):
        r = rows(i * RB, RB)
        h = row[r].astype(F32) + (dot(att[r], wmix[...]) + vecs[3:4])
        h = h - mean(h)
        rs = lax.rsqrt(mean(h * h) + EPS)
        h = h * rs
        xhat[r] = h
        rstd[r] = rs
        low[r] = (h * vecs[4:5] + vecs[5:6]).astype(B16)
        return 0
    lax.fori_loop(0, T // RB, norm_one, 0)

    loads[2].wait()
    loads[3].wait()
    dres[...] = jnp.zeros_like(dres)

    def feed(j, _):
        s = cols(j * CR, CR)
        pre = dot(low[...], wexp[:, s]) + ebias[j]
        value, slope = normal_parts(pre)
        value = value.astype(B16)
        act[:, s] = value
        gp[:, s] = slope.astype(B16)
        dres[...] += dot(value, wcon[rows(j * CR, CR)])
        return 0
    lax.fori_loop(0, FF // CR, feed, 0)

    keep = keeps[z].astype(F32)
    for kind in (COT,):
        deal(kind, 0).wait()
        for m in (1, 2, 3):
            deal(kind, m, True).wait_recv()
    sm[0] = jnp.zeros((VECS, D), F32)

    def norm_two(i, _):
        r = rows(i * BL, BL)
        h = (xhat[r] * vecs[4:5] + vecs[5:6]) + (dres[r] + vecs[6:7])
        h = h - mean(h)
        rs = lax.rsqrt(mean(h * h) + EPS)
        h = h * rs
        send[r] = jnp.where(keep > 0, h * vecs[7:8] + vecs[8:9], row[r].astype(F32)).astype(B16)
        grad = cot[r].astype(F32) * keep
        sm[0, 10:11] += jnp.sum(grad * h, axis=0, keepdims=True)
        sm[0, 11:12] += jnp.sum(grad, axis=0, keepdims=True)
        dx = grad * vecs[7:8]
        dr = rs * (dx - mean(dx) - h * mean(dx * h))
        dres[r] = dr
        dr = dr.astype(B16)
        d_ffn[r] = dr
        sm[0, 9:10] += jnp.sum(dr.astype(F32), axis=0, keepdims=True)
        return 0
    lax.fori_loop(0, T // BL, norm_two, 0)
    for m in (3, 2, 1, 0):
        deal(OUTL, m).start()

    def back_feed(j):
        s = cols(j * CR, CR)
        d_pre = (dot(d_ffn[...], wcon[rows(j * CR, CR)], NT) * gp[:, s].astype(F32)).astype(B16)
        gp[:, s] = d_pre
        dres[...] += dot(d_pre, wexp[:, s], NT)

    def back_norm():
        for q in range(FF // D):
            sm[0, 5 + q:6 + q] = jnp.sum(gp[:, q * D:(q + 1) * D].astype(F32), axis=0, keepdims=True)

        def block(i, _):
            r = rows(i * BL, BL)
            dn, h = dres[r], xhat[r]
            sm[0, 3:4] += jnp.sum(dn * h, axis=0, keepdims=True)
            sm[0, 4:5] += jnp.sum(dn, axis=0, keepdims=True)
            dx = dn * vecs[4:5]
            dr = rstd[r] * (dx - mean(dx) - h * mean(dx * h))
            dres[r] = dr
            dr = dr.astype(B16)
            d_attn[r] = dr
            sm[0, 2:3] += jnp.sum(dr.astype(F32), axis=0, keepdims=True)
            return 0
        lax.fori_loop(0, T // BL, block, 0)
        d_att[...] = dot(d_attn[...], wmix[...], NT).astype(B16)

    def back_attend(i):
        q2, k2, v2 = (qkv[:, cols(j * D + i * 2 * HEAD_DIM, 2 * HEAD_DIM)] for j in range(3))
        da2 = d_att[:, cols(i * 2 * HEAD_DIM, 2 * HEAD_DIM)]
        dqs, dks, dvs = [], [], []
        for h in range(2):
            hs = slice(h * HEAD_DIM, (h + 1) * HEAD_DIM)
            p = probs[2 * i + h]
            dp_t = dot(v2[:, hs], da2[:, hs], NT)
            pf = p.astype(F32)
            delta = jnp.sum(pf * dp_t, axis=0, keepdims=True)
            ds = (pf * (dp_t - delta)).astype(B16)
            dqs.append(dot(k2[:, hs], ds, TN))
            dks.append(dot(ds, q2[:, hs]))
            dvs.append(dot(p, da2[:, hs]))
        dq = (jnp.concatenate(dqs, axis=0) * HEAD_DIM ** -0.5).T
        dk, dv = jnp.concatenate(dks, axis=1), jnp.concatenate(dvs, axis=1)
        for j, d in enumerate((dq, dk, dv)):
            qkv[:, cols(j * D + i * 2 * HEAD_DIM, 2 * HEAD_DIM)] = d.astype(B16)

    def back_sums():
        sm[0, 0:1] = jnp.sum(qkv[:, 0:D].astype(F32), axis=0, keepdims=True)
        sm[0, 1:2] = jnp.sum(qkv[:, 2 * D:].astype(F32), axis=0, keepdims=True)

    def back_tokens(m):
        if m == 0:
            deal(OUTL, 0).wait()
            finish(OUTL)
        r = rows(others[m] * BL, BL)
        d = dres[r] + dot(qkv[r], wproj[...], NT)
        send[r] = jnp.where(keep > 0, d, cot[r].astype(F32)).astype(B16)
        deal(OUTT, m).start()

    def cp(kind, k, src, dst, dev):
        return pltpu.make_async_remote_copy(src_ref=src, dst_ref=dst, send_sem=ssem.at[kind, k],
                                            recv_sem=rsem.at[kind, k], device_id=dev, device_id_type=MESH)

    def way(k):
        par = k % 2
        f = x * (1 - par) + y * par
        d_first = (dp + (1 - par) * (2 - 4 * x) + par * (4 - 8 * y), z)
        d_last = (dp + par * (2 - 4 * x) + (1 - par) * (4 - 8 * y), z)
        return f, d_first, d_last

    keep_rows = rows(c * HR, HR)
    give_rows = rows((1 - c) * HR, HR)

    def c_core(k):
        return cp(CORE, k, part.at[k % 2, give_rows], r0.at[k], d_core)

    def c_first(k):
        f, d_first, _ = way(k)
        return cp(FIRST, k, r0.at[k, :, cols((1 - f) * HC, HC)], r1.at[k], d_first)

    def c_za(k):
        return cp(ZA, k, r1.at[k, rows(jnp.where(is0, SR, 0), 3 * SR)], za.at[k], (dp, jnp.where(is0, 1, 2)))

    def c_zb(k):
        return cp(ZB, k, r1.at[k, rows(jnp.where(is1, 2 * SR, 0), 2 * SR)], zb.at[k], (dp, jnp.where(is1, 2, 1)))

    def c_zc(k):
        return cp(ZC, k, r1.at[k, rows(jnp.where(is1, 0, 3 * SR), SR)], zc.at[k], (dp, jnp.where(is1, 0, 3)))

    def c_last(k):
        _, _, d_last = way(k)
        return cp(LAST, k, r1.at[k, rows(z * SR, SR)], fin.at[k], d_last)

    def place(k, shard, n=1):
        f, _, _ = way(k)
        return g_out.at[k, rows(c * HR + shard * SR, n * SR), cols(f * HC, HC)]

    def c_gr(k):
        return cp(GR, k, fin.at[k], place(k, z), right)

    def c_gl(k):
        return cp(GL, k, fin.at[k], place(k, z), left)

    def c_own(k):
        return pltpu.make_async_copy(fin.at[k], place(k, z), lsem.at[k])

    def c_gf(k):
        s = jnp.where(is1, 0, 3)
        return cp(GF, k, place(k, s), place(k, s), (dp, jnp.where(is1, 2, 1)))

    def c_ge(k):
        s = jnp.where(is1, 2, 0)
        return cp(GE, k, place(k, s, 2), place(k, s, 2), (dp, jnp.where(is1, 0, 3)))

    def c_agf(k):
        f, d_first, _ = way(k)
        block = g_out.at[k, keep_rows, cols(f * HC, HC)]
        return cp(AGF, k, block, block, d_first)

    def c_agc(k):
        block = g_out.at[k, keep_rows]
        return cp(AGC, k, block, block, d_core)

    def add(a, b):
        return (a.astype(F32) + b.astype(F32)).astype(B16)

    def produce(k):
        def piece(l, lc, r, rc):
            part[k % 2] = dot(l[:, cols(lc * CR, CR)], r[:, cols(rc * CC, CC)], TN).astype(B16)

        @pl.when(k < 8)
        def _():
            piece(act, k, d_ffn, 0)

        @pl.when((k >= 8) & (k < 16))
        def _():
            piece(low, (k - 8) // 4, gp, (k - 8) % 4)

        @pl.when((k >= 16) & (k < 18))
        def _():
            piece(att, k - 16, d_attn, 0)

        @pl.when(k >= 18)
        def _():
            piece(row, (k - 18) // 3, qkv, (k - 18) % 3)

    def stage(s, k):
        if s == 0:
            @pl.when(k >= 2)
            def _():
                c_core(k - 2).wait_send()
            produce(k)
            c_core(k).start()
        elif s == 1:
            c_core(k).wait_recv()
            r0[k] = add(r0[k], part[k % 2, keep_rows])
            c_first(k).start()
        elif s == 2:
            f, _, _ = way(k)
            c_first(k).wait_recv()
            r1[k] = add(r1[k], r0[k, :, cols(f * HC, HC)])

            @pl.when(end)
            def _():
                c_za(k).start()
        elif s == 3:
            @pl.when(mid)
            def _():
                c_za(k).wait_recv()
                own = rows(jnp.where(is1, SR, 0), 3 * SR)
                r1[k, own] = add(r1[k, own], za[k])
                c_zb(k).start()
        elif s == 4:
            @pl.when(mid)
            def _():
                c_zb(k).wait_recv()
                own = rows(jnp.where(is1, 0, 2 * SR), 2 * SR)
                r1[k, own] = add(r1[k, own], zb[k])
                c_zc(k).start()
        elif s == 5:
            @pl.when(end)
            def _():
                c_zc(k).wait_recv()
                own = rows(z * SR, SR)
                r1[k, own] = add(r1[k, own], zc[k])
            c_last(k).start()
        elif s == 6:
            c_last(k).wait_recv()
            fin[k] = add(r1[k, rows(z * SR, SR)], fin[k])
            c_own(k).start()

            @pl.when(z < 3)
            def _():
                c_gr(k).start()

            @pl.when(z > 0)
            def _():
                c_gl(k).start()
        elif s == 7:
            @pl.when(is1)
            def _():
                c_gr(k).wait_recv()

            @pl.when(is2)
            def _():
                c_gl(k).wait_recv()

            @pl.when(mid)
            def _():
                c_gf(k).start()
        elif s == 8:
            @pl.when(is1)
            def _():
                c_gl(k).wait_recv()

            @pl.when(is2)
            def _():
                c_gr(k).wait_recv()

            @pl.when(mid)
            def _():
                c_gf(k).wait_recv()
                c_ge(k).start()
        elif s == 9:
            @pl.when(is0)
            def _():
                c_gl(k).wait_recv()

            @pl.when(is3)
            def _():
                c_gr(k).wait_recv()

            @pl.when(end)
            def _():
                c_ge(k).wait_recv()
            c_own(k).wait()
            c_agf(k).start()
        elif s == 10:
            c_agf(k).wait_recv()
            c_agc(k).start()
        elif s == 11:
            c_agc(k).wait_recv()
            c_first(k).wait_send()
            c_last(k).wait_send()

            @pl.when(end)
            def _():
                c_za(k).wait_send()

            @pl.when(mid)
            def _():
                c_zb(k).wait_send()
                c_zc(k).wait_send()
                c_gf(k).wait_send()
                c_ge(k).wait_send()

            @pl.when(z < 3)
            def _():
                c_gr(k).wait_send()

            @pl.when(z > 0)
            def _():
                c_gl(k).wait_send()
            c_agf(k).wait_send()
            c_agc(k).wait_send()

    steps = ((d_core, None, None), (d_x, None, None), (d_y, None, None),
             ((dp, jnp.where(is0, 1, 2)), end, mid), ((dp, jnp.where(is1, 2, 1)), mid, mid), ((dp, jnp.where(is1, 0, 3)), mid, end))

    def only(cond, f):
        f() if cond is None else pl.when(cond)(f)

    def s_copy(i):
        return pltpu.make_async_remote_copy(src_ref=sm.at[i], dst_ref=smr.at[i], send_sem=smss.at[i], recv_sem=smrs.at[i],
                                            device_id=steps[i][0], device_id_type=MESH)

    def small_step(i):
        if i > 0:
            sm[i] = sm[i - 1]

            def get():
                s_copy(i - 1).wait_recv()
                sm[i] = smr[i - 1] if i == 6 else sm[i - 1] + smr[i - 1]
            only(steps[i - 1][2], get)
        if i < 6:
            only(steps[i][1], lambda: s_copy(i).start())

    def tick(t, _):
        for s in range(len(OFF) - 1, -1, -1):
            k = t - OFF[s]

            @pl.when((k >= 0) & (k < N))
            def _():
                stage(s, k)

        @pl.when(t < 8)
        def _():
            back_feed(t)

        @pl.when(t == 8)
        def _():
            back_norm()

        @pl.when((t >= 9) & (t < 15))
        def _():
            back_attend(t - 9)

        @pl.when(t == 15)
        def _():
            back_sums()
        for m in range(4):
            @pl.when(t == 16 + m)
            def _():
                back_tokens(m)
        for i in range(7):
            @pl.when(t == N + i)
            def _():
                small_step(i)
        return 0
    lax.fori_loop(0, N + OFF[-1], tick, 0)

    small_out[...] = sm[6]
    for i in range(6):
        only(steps[i][1], lambda: s_copy(i).wait_send())
    for k in (N - 2, N - 1):
        c_core(k).wait_send()
    deal(OUTT, 0).wait()
    for kind in (TOK, LIVE, COT, OUTT):
        finish(kind)
    for m in (1, 2, 3):
        deal(OUTL, m, True).wait_recv()
        deal(OUTT, m, True).wait_recv()


def run_layer(kinds, keeps, vecs, ebias, live, tokens, cot, *weights):
    blocks, BL, _ = tokens.shape
    T = blocks * BL
    V, S, H = (pl.BlockSpec(memory_space=m) for m in (pltpu.VMEM, pltpu.SMEM, pltpu.HBM))
    low16 = lambda *s: pltpu.VMEM(s, B16)
    full = lambda *s: pltpu.VMEM(s, F32)
    sem = lambda *s: pltpu.SemaphoreType.DMA(s)
    return pl.pallas_call(
        layer_kernel,
        out_shape=[jax.ShapeDtypeStruct((N, CR, CC), B16), jax.ShapeDtypeStruct((VECS, D), F32),
                   jax.ShapeDtypeStruct(tokens.shape, B16), jax.ShapeDtypeStruct(tokens.shape, B16)],
        in_specs=[S, S, V, V, V, H, H, H, H, H, H],
        out_specs=[H, V, H, H],
        scratch_shapes=[
            low16(D, 3 * D), low16(D, D), low16(D, FF), low16(FF, D),
            low16(T, D), low16(T, D), pltpu.VMEM((blocks, 1, BL), jnp.int32), low16(T, 3 * D), low16(T, D), low16(HEADS, T, T),
            low16(T, D), low16(T, FF), low16(T, FF), full(T, D), full(T, D), low16(T, D), low16(T, D), low16(T, D),
            low16(T, D), full(T, 1), full(T, T),
            low16(2, CR, CC), low16(N, HR, CC), low16(N, HR, HC), low16(N, 3 * SR, HC), low16(N, 2 * SR, HC), low16(N, SR, HC),
            low16(N, SR, HC), full(7, VECS, D), full(6, VECS, D),
            sem(KINDS, N), sem(KINDS, N), sem(N), sem(6), sem(6), sem(4), sem(5, 4), sem(5, 4), sem(5),
        ],
        compiler_params=pltpu.CompilerParams(collective_id=0, has_side_effects=True, vmem_limit_bytes=63 * 2**20),
        name="layer",
    )(kinds, keeps, vecs, ebias, live, tokens, cot, *weights)


def widen_kernel(g, contract, expand, mixing, projection):
    i = pl.program_id(0)
    for ref, first, last in ((contract, 0, 8), (expand, 8, 16), (mixing, 16, 18), (projection, 18, 24)):
        @pl.when((i >= first) & (i < last))
        def _():
            ref[...] = g[0].astype(F32)


def widen(g):
    def spec(first, count, across):
        def place(i):
            j = jnp.clip(i - first, 0, count - 1)
            return (j // across, j % across)
        return pl.BlockSpec((CR, CC), place)
    shape = lambda r, c: jax.ShapeDtypeStruct((r, c), F32)
    return pl.pallas_call(
        widen_kernel, grid=(N,),
        in_specs=[pl.BlockSpec((1, CR, CC), lambda i: (i, 0, 0))],
        out_specs=[spec(0, 8, 1), spec(8, 8, 4), spec(16, 2, 1), spec(18, 6, 3)],
        out_shape=[shape(FF, D), shape(D, FF), shape(D, D), shape(D, 3 * D)],
        compiler_params=pltpu.CompilerParams(vmem_limit_bytes=40 * 2**20),
        cost_estimate=pl.CostEstimate(flops=0, bytes_accessed=6 * N * CR * CC, transcendentals=0),
        name="widen",
    )(g)


def local(tokens, row_kinds, live_mask, keep_flag, projection, proj_bias, mixing, mix_bias, attn_gain, attn_shift,
          expand, expand_bias, contract, contract_bias, ffn_gain, ffn_shift, cotangent):
    f32 = lambda a: a.astype(F32)
    pieces = [(0, proj_bias[0]), (2, proj_bias[1]), (3, mix_bias), (4, attn_gain), (5, attn_shift), (6, contract_bias),
              (7, ffn_gain), (8, ffn_shift)]
    vecs = sum(jnp.pad(f32(v)[None], ((i, VECS - 1 - i), (0, 0))) for i, v in pieces)
    ebias = f32(expand_bias).reshape(FF // CR, 1, CR)
    g, small, layer_out, tokens_grad = run_layer(row_kinds, keep_flag, vecs, ebias, live_mask[:, None], tokens, cotangent,
                                                 projection, mixing, expand, contract)
    groups = lax.axis_size("dp") // 8
    if groups > 1:
        index = [[i + 8 * j for j in range(groups)] for i in range(8)]
        g, small = lax.psum((g, small), "dp", axis_index_groups=index)
    contract_grad, expand_grad, mixing_grad, projection_grad = widen(g)
    return (layer_out, f32(tokens_grad), projection_grad, small[:2], mixing_grad, small[2], small[3], small[4], expand_grad,
            small[5:9].reshape(-1), contract_grad, small[9], small[10], small[11])


def solution(mesh):
    data = P("dp", "blk", None)
    in_specs = (data, P("dp"), P("dp", "blk"), P("dp")) + (P(),) * 12 + (data,)
    out_specs = (data, data) + (P(),) * 12
    return jax.shard_map(local, mesh=mesh, in_specs=in_specs, out_specs=out_specs, check_vma=False)
```

time: 341 us -> 231 us (0.68)
  local copies, waits for them, and re-layouts: 66.7 us -> 15.1 us
  matrix products: 46.9 us -> 0 us
  Pallas kernels: 168 us -> 212 us
  starting transfers between devices: 22.3 us -> 0 us
  other arithmetic: 20.6 us -> 3.23 us
  waiting for transfers between devices: 11.2 us -> 0 us
    dot_general x8 -> x0, matrix products: 46.9 us -> none  [dot(): return lax.dot_general(a, b, dims, preferred_element_type=F32)]
    pallas_call x3 -> x1, Pallas kernels: 154 us -> 197 us  [run_layer(): pl.pallas_call(layer_kernel, out_shape=[jax.ShapeDtypeStruct((N, CR, CC),...]
    ppermute x15 -> x0, starting transfers between devices: 22.3 us -> none  [deal(): piece = lax.ppermute(piece, 'blk', [(i, i ^ m) for i in range(n)])]
    dynamic_update_slice x16 -> x0, local copies, waits for them, and re-layouts: 20.7 us -> none  [deal(): lax.dynamic_update_slice(out, piece, (z ^ m,) + (0,) * (blocks.ndim - 1))]
    unnamed x63 -> x7, local copies, waits for them, and re-layouts: 23 us -> 5.91 us
    ppermute x15 -> x0, waiting for transfers between devices: 11.2 us -> none  [deal(): piece = lax.ppermute(piece, 'blk', [(i, i ^ m) for i in range(n)])]
    dynamic_slice x7 -> x0, local copies, waits for them, and re-layouts: 11.1 us -> none  [the longest x5 8.65 us: deal(): piece = lax.dynamic_index_in_dim(blocks, z ^ m, 0)]
    reduce_sum x9 -> x0, other arithmetic: 8.18 us -> none  [the longest x2 3.8 us: layer_norm(): centered = hidden - row_mean]
  transfers between devices with their start and end apart: 15 -> 0, of which waited for: 2 -> 0; matrix products, arithmetic and copies ran while one was open for 21% -> 0% of each run, Pallas kernels for 8% -> 0%
where the time goes in v3:
time: 231 us
  Pallas kernels  212 us (92%)
  local copies, waits for them, and re-layouts  15.1 us (7%)
  other arithmetic  3.23 us (1%)
    pallas_call x1, Pallas kernels, run_layer(): pl.pallas_call(layer_kernel, out_shape=[jax.ShapeDtypeStruct((N, CR, CC),...  197 us
    pallas_call x1, Pallas kernels, widen(): pl.pallas_call(widen_kernel, grid=(N,), in_specs=[pl.BlockSpec((1, CR, CC...  14.8 us
    unnamed x7, local copies, waits for them, and re-layouts  5.91 us

profile of v3, /device:TPU:0, one launch (start us, length us, event | category | flops | bytes accessed | tf_op | source)
XLA Modules:
  0.0 230.8 jit_solution(7812074685496021105)
XLA Ops:
  0.6 0.8 fusion
  1.4 0.7 broadcast_in_dim.29
  2.1 0.7 broadcast_in_dim.30
  2.8 0.7 broadcast_in_dim.31
  3.5 0.7 broadcast_in_dim.32
  4.2 0.7 broadcast_in_dim.33
  4.8 0.7 broadcast_in_dim.34
  5.5 0.7 convert_add_fusion.vecs
  6.2 1.3 reshape.39
  7.5 197.1 %layer.1 = (bf16[24,384,768]{2,1,0:T(8,128)(2,1)}, f32[16,768]{1,0:T(8,128)}, bf16[4,128,768]{2,1,0:T(8,128)(2,1)}, bf16[4,128,768]{2,1,0:T(8,128)(2,1)}) custom-call(s32[4]{0:T(128)} %kinds.1, s32[4]{0:T(128)} %keeps.1, f32[16,768]{1,0:T(8,128)} %convert_add_fusion.vecs, f32[8,1,384]{2,1,0:T(1,128)} %bitcast.2, s32[4,1,128]{2,1,0:T(1,128)} %bitcast.3, ...), custom_call_target="tpu_custom_call" | custom-call | tf_op jit(solution)/shard_map/layer/pallas_call | solution.py:550
  204.6 1.5 slice_reduce_fusion
  206.2 0.0 copy-start
  206.2 5.0 %copy-done = bf16[24,384,768]{2,1,0:T(8,128)(2,1)S(1)} copy-done((bf16[24,384,768]{2,1,0:T(8,128)(2,1)S(1)}, bf16[24,384,768]{2,1,0:T(8,128)(2,1)}, u32[]{:S(2)}) %copy-start) | copy-done | bytes 14155800
  211.2 0.0 copy-start.2
  211.2 0.0 copy-start.1
  211.2 14.8 %widen.1 = (f32[3072,768]{1,0:T(8,128)}, f32[768,3072]{1,0:T(8,128)}, f32[768,768]{1,0:T(8,128)}, f32[768,2304]{1,0:T(8,128)}) custom-call(bf16[24,384,768]{2,1,0:T(8,128)(2,1)S(1)} %copy-done), custom_call_target="tpu_custom_call" | custom-call | bytes 42467328 | tf_op jit(solution)/shard_map/widen/pallas_call | solution.py:585
  225.9 0.8 slice.36
  226.7 0.6 reshape.38
  227.4 1.3 slice.32
  228.7 0.0 copy-done.2
  228.7 1.3 convert_element_type.18
  230.0 0.0 copy-done.1
  230.0 0.9 copy.32
Async XLA Ops:
  206.2 5.0 %copy-start = (bf16[24,384,768]{2,1,0:T(8,128)(2,1)S(1)}, bf16[24,384,768]{2,1,0:T(8,128)(2,1)}, u32[]{:S(2)}) copy-start(bf16[24,384,768]{2,1,0:T(8,128)(2,1)} %get-tuple-element.24.g) | copy-start | bytes 42467332
  211.2 17.5 %copy-start.2 = (bf16[4,128,768]{2,1,0:T(8,128)(2,1)S(1)}, bf16[4,128,768]{2,1,0:T(8,128)(2,1)}, u32[]{:S(2)}) copy-start(bf16[4,128,768]{2,1,0:T(8,128)(2,1)} %get-tuple-element.23) | copy-start | bytes 2359300
  211.2 18.8 %copy-start.1 = (bf16[4,128,768]{2,1,0:T(8,128)(2,1)S(1)}, bf16[4,128,768]{2,1,0:T(8,128)(2,1)}, u32[]{:S(2)}) copy-start(bf16[4,128,768]{2,1,0:T(8,128)(2,1)} %get-tuple-element.52) | copy-start | bytes 2359300

commit v4 on v3

v4 whole, which is shorter than its diff:
```python
import functools

import jax
import jax.numpy as jnp
from jax import lax
from jax.experimental import pallas as pl
from jax.experimental.pallas import tpu as pltpu
from jax.sharding import PartitionSpec as P

D = 768
FF = 3072
HEADS = 12
HEAD_DIM = 64
DOC_SHORT = 128
MESH = pl.DeviceIdType.MESH
EPS = 1e-05
NEG = -1e9
F32, B16 = jnp.float32, jnp.bfloat16
NN = (((1,), (0,)), ((), ()))
NT = (((1,), (1,)), ((), ()))
TN = (((0,), (0,)), ((), ()))

FB = 512
BR, BC = 384, 384
HR = BR // 2
SR = HR // 4
ACROSS = (D // BC, FF // BC, D // BC, 3 * D // BC)
DOWN = (FF // BR, D // BR, D // BR, D // BR)
FROM = [0]
for _down, _across in zip(DOWN, ACROSS):
    FROM.append(FROM[-1] + _down * _across)
N = FROM[-1] // 2
L_AT = (0, FF, FF + D, FF + 2 * D, FF + 3 * D)
R_AT = (0, D, D + FF, 2 * D + FF, 5 * D + FF)
KINDS = 9
CORE, FIRST, SECOND, ZA, ZB, ZC, BACK, AGF, AGC = range(KINDS)
RING = 8
PHASES = 2
OFF = [0, 2, 8, 12, 16, 20, 24, 28, 34, 36]
SMALL = [17 + 3 * i for i in range(7)]
SIDE = ((0, 6, "feed"), (6, 1, "norm"), (7, 6, "attend"), (13, 1, "sums"), (14, 4, "tokens"))
VECS = 16


def dot(a, b, dims=NN):
    return lax.dot_general(a, b, dims, preferred_element_type=F32)


def rows(start, n):
    return pl.ds(pl.multiple_of(start, 16), n)


def cols(start, n):
    return pl.ds(pl.multiple_of(start, 128), n)


def normal_parts(v):
    t = 1.0 / (1.0 + (0.3275911 * 0.5 ** 0.5) * jnp.abs(v))
    ex = jnp.exp(-0.5 * (v * v))
    poly = t * (0.127414796 + t * (-0.142248368 + t * (0.7107068705 + t * (-0.7265760135 + t * 0.5307027145))))
    tail = poly * ex
    below = jnp.where(v < 0, tail, 1.0 - tail)
    return v * below, below + v * (ex * 0.3989422804014327)


def mean(a):
    return jnp.sum(a, axis=1, keepdims=True) * (1.0 / D)


def layer_kernel(kinds, keeps, proj_bias, mix_bias, attn_gain, attn_shift, expand_bias, contract_bias, ffn_gain, ffn_shift,
                 live, tokens, cot_in, w_proj, w_mix, w_exp, w_con,
                 g_out, small_out, out_l, out_t,
                 vecs, wproj, wmix, wexp, wcon, left, right, cot, livebuf, probs, xhat, dres, d_att,
                 send, rstd, bias, held, ebuf,
                 part, r0, r1, za, zb, zc, sm, smr,
                 ssem, rsem, lsem, smss, smrs, wsem, dsend, drecv, dloc):
    dp, z = lax.axis_index("dp"), lax.axis_index("blk")
    T = left.shape[0]
    act, low, att, row = (left.at[:, a:b] for a, b in zip(L_AT, L_AT[1:]))
    d_ffn, gp, d_attn, qkv = (right.at[:, a:b] for a, b in zip(R_AT, R_AT[1:]))
    BL = T // 4
    c, x, y = dp % 2, (dp // 2) % 2, (dp // 4) % 2
    d_core = (dp + 1 - 2 * c, z)
    d_x = (dp + 2 - 4 * x, z)
    d_y = (dp + 4 - 8 * y, z)
    is0, is1 = z == 0, z == 1
    end, mid = (z == 0) | (z == 3), (z == 1) | (z == 2)
    others = (z, z + 1 - 2 * (z % 2), z + 2 - 4 * (z // 2), 3 - z)

    loads = [pltpu.make_async_copy(a, b, wsem.at[i]) for i, (a, b) in
             enumerate(((w_proj, wproj), (w_mix, wmix), (w_exp, wexp), (w_con, wcon)))]

    barrier = pltpu.get_barrier_semaphore()
    for d in (d_core, d_x, d_y) + tuple((dp, others[m]) for m in (1, 2, 3)):
        pl.semaphore_signal(barrier, inc=1, device_id=d, device_id_type=MESH)
    pl.semaphore_wait(barrier, 6)

    TOK, LIVE, COT, OUTL, OUTT = range(5)

    def deal(kind, m, arriving=False):
        there = others[m]
        src, dst = {
            TOK: lambda: (tokens.at[there], row.at[rows((there if arriving else z) * BL, BL)]),
            LIVE: lambda: (live, livebuf.at[there if arriving else z]),
            COT: lambda: (cot_in.at[there], cot.at[rows((there if arriving else z) * BL, BL)]),
            OUTL: lambda: (send.at[rows(there * BL, BL)], out_l.at[there if arriving else z]),
            OUTT: lambda: (send.at[rows(there * BL, BL)], out_t.at[there if arriving else z]),
        }[kind]()
        if m == 0:
            return pltpu.make_async_copy(src, dst, dloc.at[kind])
        return pltpu.make_async_remote_copy(src_ref=src, dst_ref=dst, send_sem=dsend.at[kind, m], recv_sem=drecv.at[kind, m],
                                            device_id=(dp, there), device_id_type=MESH)

    def finish(kind):
        for m in (1, 2, 3):
            deal(kind, m).wait_send()

    for m in (3, 2, 1, 0):
        deal(LIVE, m).start()
        deal(TOK, m).start()
    for load in loads:
        load.start()
    wide = lambda v: v[...].astype(F32).reshape(1, v.shape[0])
    vecs[0:1] = proj_bias[0:1].astype(F32)
    vecs[1:2] = jnp.zeros((1, D), F32)
    vecs[2:3] = proj_bias[1:2].astype(F32)
    for i, v in enumerate((mix_bias, attn_gain, attn_shift, contract_bias, ffn_gain, ffn_shift)):
        vecs[3 + i:4 + i] = wide(v)
    ebias = wide(expand_bias)
    for j in range(FF // FB):
        ebuf[j] = ebias[:, j * FB:(j + 1) * FB]

    def project(m):
        (deal(TOK, 0).wait if m == 0 else deal(TOK, m, True).wait_recv)()
        r = rows(others[m] * BL, BL)
        for j in range(3):
            s = slice(j * D, (j + 1) * D)
            part_j = dot(row[r], wproj[:, s]) + vecs[j:j + 1]
            if j == 0:
                part_j = part_j.astype(B16).astype(F32) * HEAD_DIM ** -0.5
            qkv[r, s] = part_j.astype(B16)

    loads[0].wait()
    for m in (0, 1, 2, 3):
        project(m)
    for m in (3, 2, 1, 0):
        deal(COT, m).start()

    deal(LIVE, 0).wait()
    for m in (1, 2, 3):
        deal(LIVE, m, True).wait_recv()
    count = jnp.sum(sum(livebuf[j, pl.ds(z, 1)] for j in range(4)), axis=1, keepdims=True)
    short = (1 - kinds[z]).astype(F32) * NEG
    for b in range(4):
        key = lax.broadcasted_iota(jnp.int32, (BL, T), 0) + b * BL
        query = lax.broadcasted_iota(jnp.int32, (BL, T), 1)
        shift = DOC_SHORT.bit_length() - 1
        apart = jnp.where((key >> shift) == (query >> shift), 0.0, short)
        bias[b * BL:(b + 1) * BL] = jnp.where(key < count, apart, NEG)

    def attend(i, _):
        s = cols(i * 2 * HEAD_DIM, 2 * HEAD_DIM)
        q2, k2, v2 = (qkv[:, cols(j * D + i * 2 * HEAD_DIM, 2 * HEAD_DIM)] for j in range(3))
        outs = []
        for h in range(2):
            hs = slice(h * HEAD_DIM, (h + 1) * HEAD_DIM)
            scores = dot(k2[:, hs], q2[:, hs], NT) + bias[...]
            e = jnp.exp(scores - jnp.max(scores, axis=0, keepdims=True))
            p = (e * (1.0 / jnp.sum(e, axis=0, keepdims=True))).astype(B16)
            probs[2 * i + h] = p
            outs.append(dot(v2[:, hs], p, TN))
        att[:, s] = jnp.concatenate(outs, axis=0).T.astype(B16)
        return 0
    lax.fori_loop(0, HEADS // 2, attend, 0)

    loads[1].wait()
    RB = 256

    def norm_one(i, _):
        r = rows(i * RB, RB)
        h = row[r].astype(F32) + (dot(att[r], wmix[...]) + vecs[3:4])
        h = h - mean(h)
        rs = lax.rsqrt(mean(h * h) + EPS)
        h = h * rs
        xhat[r] = h
        rstd[r] = rs
        low[r] = (h * vecs[4:5] + vecs[5:6]).astype(B16)
        return 0
    lax.fori_loop(0, T // RB, norm_one, 0)

    loads[2].wait()
    loads[3].wait()
    dres[...] = jnp.zeros_like(dres)

    def feed(j, _):
        s = cols(j * FB, FB)
        pre = dot(low[...], wexp[:, s]) + ebuf[j]
        value, slope = normal_parts(pre)
        value = value.astype(B16)
        act[:, s] = value
        gp[:, s] = slope.astype(B16)
        dres[...] += dot(value, wcon[rows(j * FB, FB)])
        return 0
    lax.fori_loop(0, FF // FB, feed, 0)

    keep = keeps[z].astype(F32)
    for kind in (COT,):
        deal(kind, 0).wait()
        for m in (1, 2, 3):
            deal(kind, m, True).wait_recv()
    sm[0] = jnp.zeros((VECS, D), F32)

    def norm_two(i, _):
        r = rows(i * BL, BL)
        h = (xhat[r] * vecs[4:5] + vecs[5:6]) + (dres[r] + vecs[6:7])
        h = h - mean(h)
        rs = lax.rsqrt(mean(h * h) + EPS)
        h = h * rs
        send[r] = jnp.where(keep > 0, h * vecs[7:8] + vecs[8:9], row[r].astype(F32)).astype(B16)
        grad = cot[r].astype(F32) * keep
        sm[0, 10:11] += jnp.sum(grad * h, axis=0, keepdims=True)
        sm[0, 11:12] += jnp.sum(grad, axis=0, keepdims=True)
        dx = grad * vecs[7:8]
        dr = rs * (dx - mean(dx) - h * mean(dx * h))
        dres[r] = dr
        dr = dr.astype(B16)
        d_ffn[r] = dr
        sm[0, 9:10] += jnp.sum(dr.astype(F32), axis=0, keepdims=True)
        return 0
    lax.fori_loop(0, T // BL, norm_two, 0)
    for m in (3, 2, 1, 0):
        deal(OUTL, m).start()

    def back_feed(j, step):
        s = cols(j * FB, FB)
        if step == 0:
            gp[:, s] = (dot(d_ffn[...], wcon[rows(j * FB, FB)], NT) * gp[:, s].astype(F32)).astype(B16)
        else:
            dres[...] += dot(gp[:, s], wexp[:, s], NT)

    def back_norm(_, step):
        if step == 1:
            d_att[...] = dot(d_attn[...], wmix[...], NT).astype(B16)
            return
        for q in range(FF // D):
            sm[0, 5 + q:6 + q] = jnp.sum(gp[:, q * D:(q + 1) * D].astype(F32), axis=0, keepdims=True)

        def block(i, _):
            r = rows(i * BL, BL)
            dn, h = dres[r], xhat[r]
            sm[0, 3:4] += jnp.sum(dn * h, axis=0, keepdims=True)
            sm[0, 4:5] += jnp.sum(dn, axis=0, keepdims=True)
            dx = dn * vecs[4:5]
            dr = rstd[r] * (dx - mean(dx) - h * mean(dx * h))
            dres[r] = dr
            dr = dr.astype(B16)
            d_attn[r] = dr
            sm[0, 2:3] += jnp.sum(dr.astype(F32), axis=0, keepdims=True)
            return 0
        lax.fori_loop(0, T // BL, block, 0)

    def back_attend(i, step):
        at = [cols(j * D + i * 2 * HEAD_DIM, 2 * HEAD_DIM) for j in range(3)]
        hs = slice(step * HEAD_DIM, (step + 1) * HEAD_DIM)
        q1, k1, v1 = (qkv[:, s][:, hs] for s in at)
        da1 = d_att[:, at[0]][:, hs]
        p = probs[2 * i + step]
        dp_t = dot(v1, da1, NT)
        pf = p.astype(F32)
        delta = jnp.sum(pf * dp_t, axis=0, keepdims=True)
        ds = (pf * (dp_t - delta)).astype(B16)
        dq = (dot(k1, ds, TN) * HEAD_DIM ** -0.5).T
        dk, dv = dot(ds, q1), dot(p, da1)
        for j, d in enumerate((dq, dk, dv)):
            if step == 0:
                held[j] = d.astype(B16)
            else:
                qkv[:, at[j]] = jnp.concatenate([held[j], d.astype(B16)], axis=1)

    def back_sums(_, step):
        if step:
            return
        sm[0, 0:1] = jnp.sum(qkv[:, 0:D].astype(F32), axis=0, keepdims=True)
        sm[0, 1:2] = jnp.sum(qkv[:, 2 * D:].astype(F32), axis=0, keepdims=True)

    def back_tokens(i, step):
        for m in range(4) if step == 0 else ():
            @pl.when(i == m)
            def _():
                if m == 0:
                    deal(OUTL, 0).wait()
                    finish(OUTL)
                r = rows(others[m] * BL, BL)
                d = dres[r] + dot(qkv[r], wproj[...], NT)
                send[r] = jnp.where(keep > 0, d, cot[r].astype(F32)).astype(B16)
                deal(OUTT, m).start()

    def cp(kind, k, src, dst, dev):
        return pltpu.make_async_remote_copy(src_ref=src, dst_ref=dst, send_sem=ssem.at[kind, k % RING],
                                            recv_sem=rsem.at[kind, k % RING], device_id=dev, device_id_type=MESH)

    def way(k):
        par = k % 2
        f = x * (1 - par) + y * par
        d_first = (dp + (1 - par) * (2 - 4 * x) + par * (4 - 8 * y), z)
        d_last = (dp + par * (2 - 4 * x) + (1 - par) * (4 - 8 * y), z)
        return f, d_first, d_last

    def c_core(k):
        return cp(CORE, k, part.at[k % 2, 1 - c], r0.at[k], d_core)

    def c_first(k):
        f, d_first, _ = way(k)
        return cp(FIRST, k, r0.at[k, rows((1 - f) * HR, HR)], r1.at[k], d_first)

    def place(k, shard, n=1):
        f, _, _ = way(k)
        return g_out.at[2 * k + c, rows(f * HR + shard * SR, n * SR)]

    def half(k):
        par = k % 2
        return y * (1 - par) + x * par

    def own_half(k):
        return rows(half(k) * 2 * SR, 2 * SR)

    def f_second(k):
        _, _, d_last = way(k)
        return cp(SECOND, k, r1.at[k, rows((1 - half(k)) * 2 * SR, 2 * SR)], za.at[k], d_last)

    def f_za(k):
        return cp(ZA, k, r1.at[k, own_half(k)], zb.at[k], (dp, jnp.where(is0, 1, 2)))

    def f_zb(k):
        return cp(ZB, k, r1.at[k, own_half(k)], zc.at[k], (dp, jnp.where(is1, 2, 1)))

    def f_place(k):
        return place(k, 2 * half(k), 2)

    def f_zc(k):
        return cp(ZC, k, za.at[k], f_place(k), (dp, jnp.where(is1, 0, 3)))

    def f_own(k):
        return pltpu.make_async_copy(za.at[k], f_place(k), lsem.at[k % RING])

    def f_back(k, from_place):
        _, _, d_last = way(k)
        return cp(BACK, k, f_place(k) if from_place else za.at[k], f_place(k), d_last)

    def f_back_in(k):
        _, _, d_last = way(k)
        there = place(k, 2 * (1 - half(k)), 2)
        return cp(BACK, k, there, there, d_last)

    def c_agf(k):
        f, d_first, _ = way(k)
        block = g_out.at[2 * k + c, rows(f * HR, HR)]
        return cp(AGF, k, block, block, d_first)

    def c_agc(k):
        block = g_out.at[2 * k + c]
        return cp(AGC, k, block, block, d_core)

    def add(a, b):
        return (a.astype(F32) + b.astype(F32)).astype(B16)

    def produce(k):
        l, r = 0, 0
        for first, across, la, ra in zip(FROM, ACROSS, L_AT, R_AT):
            at = 2 * k - first
            l = jnp.where(at >= 0, la + at // across * BR, l)
            r = jnp.where(at >= 0, ra + at % across * BC, r)
        both = dot(left[:, cols(l, BR)], right[:, cols(r, 2 * BC)], TN).astype(B16)
        for i in range(2):
            part[k % 2, i] = both[:, i * BC:(i + 1) * BC]

    def stage(s, k):
        f, _, _ = way(k)
        if s == 0:
            produce(k)
            c_core(k).start()
        elif s == 1:
            c_core(k).wait()
            r0[k] = add(r0[k], part[k % 2, c])
            c_first(k).start()
        elif s == 2:
            c_first(k).wait()
            r1[k] = add(r1[k], r0[k, rows(f * HR, HR)])
            f_second(k).start()
        elif s == 3:
            f_second(k).wait()
            r1[k, own_half(k)] = add(r1[k, own_half(k)], za[k])

            @pl.when(end)
            def _():
                f_za(k).start()
        elif s == 4:
            @pl.when(mid)
            def _():
                f_za(k).wait_recv()
                r1[k, own_half(k)] = add(r1[k, own_half(k)], zb[k])
                f_zb(k).start()
        elif s == 5:
            @pl.when(mid)
            def _():
                f_zb(k).wait()
                za[k] = add(r1[k, own_half(k)], zc[k])
                f_zc(k).start()
                f_back(k, False).start()
                f_own(k).start()
        elif s == 6:
            @pl.when(end)
            def _():
                f_zc(k).wait_recv()
                f_back(k, True).start()
                f_za(k).wait_send()
        elif s == 7:
            f_back_in(k).wait_recv()
            f_back(k, True).wait_send()

            @pl.when(mid)
            def _():
                f_own(k).wait()
                f_zc(k).wait_send()
            c_agf(k).start()
        elif s == 8:
            c_agf(k).wait()
            c_agc(k).start()
        elif s == 9:
            c_agc(k).wait()

    steps = ((d_core, None, None), (d_x, None, None), (d_y, None, None),
             ((dp, jnp.where(is0, 1, 2)), end, mid), ((dp, jnp.where(is1, 2, 1)), mid, mid), ((dp, jnp.where(is1, 0, 3)), mid, end))

    def only(cond, f):
        f() if cond is None else pl.when(cond)(f)

    def s_copy(i):
        return pltpu.make_async_remote_copy(src_ref=sm.at[i], dst_ref=smr.at[i], send_sem=smss.at[i], recv_sem=smrs.at[i],
                                            device_id=steps[i][0], device_id_type=MESH)

    def small_step(i):
        if i > 0:
            sm[i] = sm[i - 1]

            def get():
                s_copy(i - 1).wait_recv()
                sm[i] = smr[i - 1] if i == 6 else sm[i - 1] + smr[i - 1]
            only(steps[i - 1][2], get)
        if i < 6:
            only(steps[i][1], lambda: s_copy(i).start())

    def tick(t, _):
        works = {"feed": back_feed, "norm": back_norm, "attend": back_attend, "sums": back_sums, "tokens": back_tokens}
        for phase in range(PHASES):
            for s in range(len(OFF) - 1, -1, -1):
                if OFF[s] % PHASES == phase:
                    k = t - OFF[s] // PHASES

                    @pl.when((k >= 0) & (k < N))
                    def _():
                        stage(s, k)
            for step in range(phase * 2 // PHASES, (phase + 1) * 2 // PHASES):
                for first, count, work in SIDE:
                    @pl.when((t >= first) & (t < first + count))
                    def _():
                        works[work](t - first, step)
        for i in range(7):
            @pl.when(t == SMALL[i])
            def _():
                small_step(i)
        return 0
    lax.fori_loop(0, N + OFF[-1] // PHASES, tick, 0)

    small_out[...] = sm[6]
    for i in range(6):
        only(steps[i][1], lambda: s_copy(i).wait_send())
    deal(OUTT, 0).wait()
    for kind in (TOK, LIVE, COT, OUTT):
        finish(kind)
    for m in (1, 2, 3):
        deal(OUTL, m, True).wait_recv()
        deal(OUTT, m, True).wait_recv()


def run_layer(kinds, keeps, *rest):
    tokens = rest[9]
    blocks, BL, _ = tokens.shape
    T = blocks * BL
    V, S, H = (pl.BlockSpec(memory_space=m) for m in (pltpu.VMEM, pltpu.SMEM, pltpu.HBM))
    low16 = lambda *s: pltpu.VMEM(s, B16)
    full = lambda *s: pltpu.VMEM(s, F32)
    sem = lambda *s: pltpu.SemaphoreType.DMA(s)
    return pl.pallas_call(
        layer_kernel,
        out_shape=[jax.ShapeDtypeStruct((2 * N, BR, BC), B16), jax.ShapeDtypeStruct((VECS, D), F32),
                   jax.ShapeDtypeStruct(tokens.shape, B16), jax.ShapeDtypeStruct(tokens.shape, B16)],
        in_specs=[S, S] + [V] * 9 + [H] * 6,
        out_specs=[H, V, H, H],
        scratch_shapes=[
            full(VECS, D), low16(D, 3 * D), low16(D, D), low16(D, FF), low16(FF, D),
            low16(T, L_AT[-1]), low16(T, R_AT[-1]), low16(T, D), pltpu.VMEM((blocks, blocks, BL), jnp.int32), low16(HEADS, T, T),
            full(T, D), full(T, D), low16(T, D),
            low16(T, D), full(T, 1), full(T, T), low16(3, T, HEAD_DIM), full(FF // FB, 1, FB),
            low16(2, 2, BR, BC), low16(N, BR, BC), low16(N, HR, BC), low16(N, 2 * SR, BC), low16(N, 2 * SR, BC),
            low16(N, 2 * SR, BC), full(7, VECS, D), full(6, VECS, D),
            sem(KINDS, RING), sem(KINDS, RING), sem(RING), sem(6), sem(6), sem(4), sem(5, 4), sem(5, 4), sem(5),
        ],
        compiler_params=pltpu.CompilerParams(collective_id=0, has_side_effects=True, vmem_limit_bytes=63 * 2**20),
        name="layer",
    )(kinds, keeps, *rest)


AHEAD = 4


def widen_kernel(g, small, out_l, out_t, layer_out, tokens_grad, projection, proj_bias, mixing, mix_bias, attn_gain, attn_shift,
                 expand, expand_bias, contract, contract_bias, ffn_gain, ffn_shift, low, wide, tin, tout, lin, isem, osem, tsem):
    def come(k):
        return pltpu.make_async_copy(g.at[pl.ds(2 * k, 2)], low.at[k], isem.at[k])

    def go(k, ref, at, across):
        return pltpu.make_async_copy(wide.at[k], ref.at[rows(at // across * BR, BR), cols(at % across * 2 * BC, 2 * BC)], osem.at[k])

    t_in, t_out = pltpu.make_async_copy(out_t, tin, tsem.at[0]), pltpu.make_async_copy(tout, tokens_grad, tsem.at[1])
    l_in, l_out = pltpu.make_async_copy(out_l, lin, tsem.at[2]), pltpu.make_async_copy(lin, layer_out, tsem.at[3])
    t_in.start()
    l_in.start()
    for k in range(AHEAD):
        come(k).start()
    grads = list(zip((contract, expand, mixing, projection), FROM, FROM[1:], ACROSS))
    for ref, first, last, across in grads:
        def step(k, _):
            @pl.when(k + AHEAD < N)
            def _():
                come(k + AHEAD).start()
            come(k).wait()
            for i in range(2):
                wide[k, :, i * BC:(i + 1) * BC] = low[k, i].astype(F32)
            go(k, ref, k - first // 2, across // 2).start()
            return 0
        lax.fori_loop(first // 2, last // 2, step, 0)
    l_in.wait()
    l_out.start()
    t_in.wait()
    tout[...] = tin[...].astype(F32)
    t_out.start()
    proj_bias[...] = small[0:2]
    for i, ref in ((2, mix_bias), (3, attn_gain), (4, attn_shift), (9, contract_bias), (10, ffn_gain), (11, ffn_shift)):
        ref[...] = small[i:i + 1].reshape(D)
    for q in range(FF // D):
        expand_bias[q * D:(q + 1) * D] = small[5 + q:6 + q].reshape(D)
    l_out.wait()
    t_out.wait()
    for ref, first, last, across in grads:
        def done(k, _):
            go(k, ref, k - first // 2, across // 2).wait()
            return 0
        lax.fori_loop(first // 2, last // 2, done, 0)


def widen(g, small, out_l, out_t):
    V, H = (pl.BlockSpec(memory_space=m) for m in (pltpu.VMEM, pltpu.HBM))
    shape = lambda *s: jax.ShapeDtypeStruct(s, F32)
    vec = shape(D)
    return pl.pallas_call(
        widen_kernel,
        in_specs=[H, V, H, H],
        out_specs=[H, H, H, V, H, V, V, V, H, V, H, V, V, V],
        out_shape=[jax.ShapeDtypeStruct(out_l.shape, B16), shape(*out_t.shape), shape(D, 3 * D), shape(2, D), shape(D, D),
                   vec, vec, vec, shape(D, FF), shape(FF), shape(FF, D), vec, vec, vec],
        scratch_shapes=[pltpu.VMEM((N, 2, BR, BC), B16), pltpu.VMEM((N, BR, 2 * BC), F32), pltpu.VMEM(out_t.shape, B16),
                        pltpu.VMEM(out_t.shape, F32), pltpu.VMEM(out_l.shape, B16)] + [pltpu.SemaphoreType.DMA((n,)) for n in (N, N, 4)],
        compiler_params=pltpu.CompilerParams(vmem_limit_bytes=60 * 2**20),
        cost_estimate=pl.CostEstimate(flops=0, bytes_accessed=12 * N * BR * BC, transcendentals=0),
        name="widen",
    )(g, small, out_l, out_t)


def local(tokens, row_kinds, live_mask, keep_flag, projection, proj_bias, mixing, mix_bias, attn_gain, attn_shift,
          expand, expand_bias, contract, contract_bias, ffn_gain, ffn_shift, cotangent):
    g, small, layer_out, tokens_grad = run_layer(
        row_kinds, keep_flag, proj_bias, mix_bias, attn_gain, attn_shift, expand_bias, contract_bias, ffn_gain, ffn_shift,
        live_mask, tokens, cotangent, projection, mixing, expand, contract)
    groups = lax.axis_size("dp") // 8
    if groups > 1:
        index = [[i + 8 * j for j in range(groups)] for i in range(8)]
        g, small = lax.psum((g, small), "dp", axis_index_groups=index)
    return tuple(widen(g, small, layer_out, tokens_grad))


def solution(mesh):
    data = P("dp", "blk", None)
    in_specs = (data, P("dp"), P("dp", "blk"), P("dp")) + (P(),) * 12 + (data,)
    out_specs = (data, data) + (P(),) * 12
    return jax.shard_map(local, mesh=mesh, in_specs=in_specs, out_specs=out_specs, check_vma=False)
```

time: 231 us -> 201 us (0.87)
  local copies, waits for them, and re-layouts: 15.1 us -> 0 us
  Pallas kernels: 212 us -> 200 us
  other arithmetic: 3.23 us -> 0 us
    pallas_call x2, Pallas kernels: 212 us -> 200 us  [the longest x1 182 us: run_layer(): pl.pallas_call(layer_kernel, out_shape=[jax.ShapeDtypeStruct((2 * N, BR,...]
    unnamed x7 -> x0, local copies, waits for them, and re-layouts: 5.91 us -> none
    slice x4 -> x0, local copies, waits for them, and re-layouts: 4.45 us -> none  [the longest x1 1.54 us: local(): small[11]]
    broadcast_in_dim x6 -> x0, local copies, waits for them, and re-layouts: 4.11 us -> none  [local(): f32(v)[None]]
where the time goes in v4:
time: 201 us
  Pallas kernels  200 us (100%)
    pallas_call x1, Pallas kernels, run_layer(): pl.pallas_call(layer_kernel, out_shape=[jax.ShapeDtypeStruct((2 * N, BR,...  182 us
    pallas_call x1, Pallas kernels, widen(): pl.pallas_call(widen_kernel, in_specs=[H, V, H, H], out_specs=[H, H, H, V...  17.4 us

profile of v4, /device:TPU:0, one launch (start us, length us, event | category | flops | bytes accessed | tf_op | source)
XLA Modules:
  0.0 200.7 jit_solution(2396906971165109689)
XLA Ops:
  0.7 182.4 %layer.1 = (bf16[48,384,384]{2,1,0:T(8,128)(2,1)}, f32[16,768]{1,0:T(8,128)}, bf16[4,128,768]{2,1,0:T(8,128)(2,1)}, bf16[4,128,768]{2,1,0:T(8,128)(2,1)}) custom-call(s32[4]{0:T(128)} %kinds.1, s32[4]{0:T(128)} %keeps.1, bf16[2,768]{1,0:T(2,128)(2,1)} %proj_bias.1, bf16[768]{0:T(1024)(128)(2,1)} %mix_bias.1, bf16[768]{0:T(1024)(128)(2,1)} %attn_gain.1, ...), custom_call_target="tpu_custom_call" | custom-call | tf_op jit(solution)/shard_map/layer/pallas_call | solution.py:494
  183.1 17.4 %widen.1 = (bf16[4,128,768]{2,1,0:T(8,128)(2,1)}, f32[4,128,768]{2,1,0:T(8,128)}, f32[768,2304]{1,0:T(8,128)}, f32[2,768]{1,0:T(2,128)}, f32[768,768]{1,0:T(8,12...) custom-call(bf16[48,384,384]{2,1,0:T(8,128)(2,1)} %get-tuple-element, ...), custom_call_target="tpu_custom_call" | custom-call | bytes 42467328 | tf_op jit(solution)/shard_map/widen/pallas_call | solution.py:566

commit v5 on v4

--- a/solution.py
+++ b/solution.py
@@ -32,11 +32,13 @@
 N = FROM[-1] // 2
 L_AT = (0, FF, FF + D, FF + 2 * D, FF + 3 * D)
 R_AT = (0, D, D + FF, 2 * D + FF, 5 * D + FF)
-KINDS = 9
-CORE, FIRST, SECOND, ZA, ZB, ZC, BACK, AGF, AGC = range(KINDS)
+KINDS = 15
+CORE, FIRST, SECOND, ZA, ZB, ZC, BACK, AGF, AGC, MID, TOEND, I_ZA, I_ZB, I_ZC, I_SECOND = range(KINDS)
+INNER = (10, 18)
 RING = 8
 PHASES = 2
-OFF = [0, 2, 8, 12, 16, 20, 24, 28, 34, 36]
+OFF = [0, 2, 8, 12, 16, 20, 24, 28, 34, 38]
+OFF_INNER = [0, 2, 8, 13, 17, 21, 25, 29, 35, 39]
 SMALL = [17 + 3 * i for i in range(7)]
 SIDE = ((0, 6, "feed"), (6, 1, "norm"), (7, 6, "attend"), (13, 1, "sums"), (14, 4, "tokens"))
 VECS = 16
@@ -158,7 +160,7 @@
         apart = jnp.where((key >> shift) == (query >> shift), 0.0, short)
         bias[b * BL:(b + 1) * BL] = jnp.where(key < count, apart, NEG)
 
-    def attend(i, _):
+    def attend_pair(i):
         s = cols(i * 2 * HEAD_DIM, 2 * HEAD_DIM)
         q2, k2, v2 = (qkv[:, cols(j * D + i * 2 * HEAD_DIM, 2 * HEAD_DIM)] for j in range(3))
         outs = []
@@ -170,8 +172,11 @@
             probs[2 * i + h] = p
             outs.append(dot(v2[:, hs], p, TN))
         att[:, s] = jnp.concatenate(outs, axis=0).T.astype(B16)
+    def attend(i, _):
+        for j in range(2):
+            attend_pair(i * 2 + j)
         return 0
-    lax.fori_loop(0, HEADS // 2, attend, 0)
+    lax.fori_loop(0, HEADS // 4, attend, 0)
 
     loads[1].wait()
     RB = 256
@@ -194,12 +199,14 @@
 
     def feed(j, _):
         s = cols(j * FB, FB)
-        pre = dot(low[...], wexp[:, s]) + ebuf[j]
-        value, slope = normal_parts(pre)
-        value = value.astype(B16)
-        act[:, s] = value
-        gp[:, s] = slope.astype(B16)
-        dres[...] += dot(value, wcon[rows(j * FB, FB)])
+        parts = [slice(i * T // 2, (i + 1) * T // 2) for i in range(2)]
+        pres = [dot(low[p, :], wexp[:, s]) + ebuf[j] for p in parts]
+        for p, pre in zip(parts, pres):
+            value, slope = normal_parts(pre)
+            value = value.astype(B16)
+            act[p, s] = value
+            gp[p, s] = slope.astype(B16)
+            dres[p, :] += dot(value, wcon[rows(j * FB, FB)])
         return 0
     lax.fori_loop(0, FF // FB, feed, 0)
 
@@ -326,7 +333,7 @@
 
     def f_second(k):
         _, _, d_last = way(k)
-        return cp(SECOND, k, r1.at[k, rows((1 - half(k)) * 2 * SR, 2 * SR)], za.at[k], d_last)
+        return cp(SECOND, k, r1.at[k, rows((1 - half(k)) * 2 * SR, 2 * SR)], za.at[k, rows(0, 2 * SR)], d_last)
 
     def f_za(k):
         return cp(ZA, k, r1.at[k, own_half(k)], zb.at[k], (dp, jnp.where(is0, 1, 2)))
@@ -338,19 +345,45 @@
         return place(k, 2 * half(k), 2)
 
     def f_zc(k):
-        return cp(ZC, k, za.at[k], f_place(k), (dp, jnp.where(is1, 0, 3)))
+        return cp(ZC, k, za.at[k, rows(0, 2 * SR)], f_place(k), (dp, jnp.where(is1, 0, 3)))
 
     def f_own(k):
-        return pltpu.make_async_copy(za.at[k], f_place(k), lsem.at[k % RING])
+        return pltpu.make_async_copy(za.at[k, rows(0, 2 * SR)], f_place(k), lsem.at[k % RING])
 
     def f_back(k, from_place):
         _, _, d_last = way(k)
-        return cp(BACK, k, f_place(k) if from_place else za.at[k], f_place(k), d_last)
+        return cp(BACK, k, f_place(k) if from_place else za.at[k, rows(0, 2 * SR)], f_place(k), d_last)
 
     def f_back_in(k):
         _, _, d_last = way(k)
         there = place(k, 2 * (1 - half(k)), 2)
         return cp(BACK, k, there, there, d_last)
+
+    side = jnp.where(z < 2, 0, 1)
+    mine, theirs = rows(side * 2 * SR, 2 * SR), rows((1 - side) * 2 * SR, 2 * SR)
+
+    def i_za(k):
+        return cp(I_ZA, k, r1.at[k], za.at[k], (dp, jnp.where(is0, 1, 2)))
+
+    def i_zb(k):
+        return cp(I_ZB, k, r1.at[k, theirs], zb.at[k], (dp, jnp.where(is1, 2, 1)))
+
+    def i_second(k):
+        _, _, d_last = way(k)
+        return cp(I_SECOND, k, r1.at[k, mine], zc.at[k], d_last)
+
+    def i_own(k):
+        return pltpu.make_async_copy(za.at[k, rows(0, 2 * SR)], place(k, 2 * side, 2), lsem.at[k % RING])
+
+    def i_mid(k):
+        return cp(MID, k, za.at[k, rows(0, 2 * SR)], place(k, 2 * side, 2), (dp, jnp.where(is1, 2, 1)))
+
+    def i_end(k):
+        return cp(I_ZC, k, za.at[k, rows(0, 2 * SR)], place(k, 2 * side, 2), (dp, jnp.where(is1, 0, 3)))
+
+    def i_end_too(k):
+        there = place(k, 2 * (1 - side), 2)
+        return cp(TOEND, k, there, there, (dp, jnp.where(is1, 0, 3)))
 
     def c_agf(k):
         f, d_first, _ = way(k)
@@ -374,8 +407,7 @@
         for i in range(2):
             part[k % 2, i] = both[:, i * BC:(i + 1) * BC]
 
-    def stage(s, k):
-        f, _, _ = way(k)
+    def stage_both(s, k):
         if s == 0:
             produce(k)
             c_core(k).start()
@@ -383,13 +415,16 @@
             c_core(k).wait()
             r0[k] = add(r0[k], part[k % 2, c])
             c_first(k).start()
-        elif s == 2:
+
+    def stage_flat(s, k):
+        f, _, _ = way(k)
+        if s == 2:
             c_first(k).wait()
             r1[k] = add(r1[k], r0[k, rows(f * HR, HR)])
             f_second(k).start()
         elif s == 3:
             f_second(k).wait()
-            r1[k, own_half(k)] = add(r1[k, own_half(k)], za[k])
+            r1[k, own_half(k)] = add(r1[k, own_half(k)], za[k, :2 * SR])
 
             @pl.when(end)
             def _():
@@ -404,7 +439,7 @@
             @pl.when(mid)
             def _():
                 f_zb(k).wait()
-                za[k] = add(r1[k, own_half(k)], zc[k])
+                za[k, :2 * SR] = add(r1[k, own_half(k)], zc[k])
                 f_zc(k).start()
                 f_back(k, False).start()
                 f_own(k).start()
@@ -429,6 +464,65 @@
         elif s == 9:
             c_agc(k).wait()
 
+    def stage_inner(s, k):
+        f, _, _ = way(k)
+        if s == 2:
+            c_first(k).wait()
+            r1[k] = add(r1[k], r0[k, rows(f * HR, HR)])
+
+            @pl.when(end)
+            def _():
+                i_za(k).start()
+        elif s == 3:
+            @pl.when(mid)
+            def _():
+                i_za(k).wait_recv()
+                r1[k] = add(r1[k], za[k])
+                i_zb(k).start()
+        elif s == 4:
+            @pl.when(mid)
+            def _():
+                i_zb(k).wait()
+                r1[k, mine] = add(r1[k, mine], zb[k])
+                i_second(k).start()
+
+            @pl.when(end)
+            def _():
+                i_za(k).wait_send()
+        elif s == 5:
+            @pl.when(mid)
+            def _():
+                i_second(k).wait()
+                za[k, :2 * SR] = add(r1[k, mine], zc[k])
+                i_mid(k).start()
+                i_end(k).start()
+                i_own(k).start()
+        elif s == 6:
+            @pl.when(mid)
+            def _():
+                i_mid(k).wait()
+                i_end_too(k).start()
+        elif s == 7:
+            @pl.when(mid)
+            def _():
+                i_own(k).wait()
+                i_end(k).wait_send()
+
+            @pl.when(end)
+            def _():
+                i_end(k).wait_recv()
+                i_end_too(k).wait_recv()
+            c_agf(k).start()
+        elif s == 8:
+            c_agf(k).wait()
+            c_agc(k).start()
+
+            @pl.when(mid)
+            def _():
+                i_end_too(k).wait_send()
+        elif s == 9:
+            c_agc(k).wait()
+
     steps = ((d_core, None, None), (d_x, None, None), (d_y, None, None),
              ((dp, jnp.where(is0, 1, 2)), end, mid), ((dp, jnp.where(is1, 2, 1)), mid, mid), ((dp, jnp.where(is1, 0, 3)), mid, end))
 
@@ -453,13 +547,20 @@
     def tick(t, _):
         works = {"feed": back_feed, "norm": back_norm, "attend": back_attend, "sums": back_sums, "tokens": back_tokens}
         for phase in range(PHASES):
-            for s in range(len(OFF) - 1, -1, -1):
-                if OFF[s] % PHASES == phase:
-                    k = t - OFF[s] // PHASES
-
-                    @pl.when((k >= 0) & (k < N))
+            def run(stage, s, after, wanted):
+                if after % PHASES == phase:
+                    k = t - after // PHASES
+
+                    @pl.when(wanted(k))
                     def _():
                         stage(s, k)
+            inner = lambda k: (k >= INNER[0]) & (k < INNER[1])
+            flat = lambda k: ((k >= 0) & (k < INNER[0])) | ((k >= INNER[1]) & (k < N))
+            for s in range(len(OFF) - 1, 1, -1):
+                run(stage_flat, s, OFF[s], flat)
+                run(stage_inner, s, OFF_INNER[s], inner)
+            for s in (1, 0):
+                run(stage_both, s, OFF[s], lambda k: (k >= 0) & (k < N))
             for step in range(phase * 2 // PHASES, (phase + 1) * 2 // PHASES):
                 for first, count, work in SIDE:
                     @pl.when((t >= first) & (t < first + count))
@@ -470,7 +571,7 @@
             def _():
                 small_step(i)
         return 0
-    lax.fori_loop(0, N + OFF[-1] // PHASES, tick, 0)
+    lax.fori_loop(0, N + max(OFF[-1], OFF_INNER[-1]) // PHASES, tick, 0)
 
     small_out[...] = sm[6]
     for i in range(6):
@@ -502,7 +603,7 @@
             low16(T, L_AT[-1]), low16(T, R_AT[-1]), low16(T, D), pltpu.VMEM((blocks, blocks, BL), jnp.int32), low16(HEADS, T, T),
             full(T, D), full(T, D), low16(T, D),
             low16(T, D), full(T, 1), full(T, T), low16(3, T, HEAD_DIM), full(FF // FB, 1, FB),
-            low16(2, 2, BR, BC), low16(N, BR, BC), low16(N, HR, BC), low16(N, 2 * SR, BC), low16(N, 2 * SR, BC),
+            low16(2, 2, BR, BC), low16(N, BR, BC), low16(N, HR, BC), low16(N, HR, BC), low16(N, 2 * SR, BC),
             low16(N, 2 * SR, BC), full(7, VECS, D), full(6, VECS, D),
             sem(KINDS, RING), sem(KINDS, RING), sem(RING), sem(6), sem(6), sem(4), sem(5, 4), sem(5, 4), sem(5),
         ],

time: 201 us -> 196 us (0.975)
  Pallas kernels: 200 us -> 195 us
    pallas_call x1, Pallas kernels: 182 us -> 177 us  [run_layer(): pl.pallas_call(layer_kernel, out_shape=[jax.ShapeDtypeStruct((2 * N, BR,...]
where the time goes in v5:
time: 196 us; the launch traced here: 195 us
  Pallas kernels  195 us (99%)
    pallas_call x1, Pallas kernels, run_layer(): pl.pallas_call(layer_kernel, out_shape=[jax.ShapeDtypeStruct((2 * N, BR,...  177 us
    pallas_call x1, Pallas kernels, widen(): pl.pallas_call(widen_kernel, in_specs=[H, V, H, H], out_specs=[H, H, H, V...  17.4 us

profile of v5, /device:TPU:0, one launch (start us, length us, event | category | flops | bytes accessed | tf_op | source)
XLA Modules:
  0.0 195.5 jit_solution(3966246260019093989)
XLA Ops:
  0.7 177.2 %layer.1 = (bf16[48,384,384]{2,1,0:T(8,128)(2,1)}, f32[16,768]{1,0:T(8,128)}, bf16[4,128,768]{2,1,0:T(8,128)(2,1)}, bf16[4,128,768]{2,1,0:T(8,128)(2,1)}) custom-call(s32[4]{0:T(128)} %kinds.1, s32[4]{0:T(128)} %keeps.1, bf16[2,768]{1,0:T(2,128)(2,1)} %proj_bias.1, bf16[768]{0:T(1024)(128)(2,1)} %mix_bias.1, bf16[768]{0:T(1024)(128)(2,1)} %attn_gain.1, ...), custom_call_target="tpu_custom_call" | custom-call | tf_op jit(solution)/shard_map/layer/pallas_call | solution.py:595
  177.9 17.4 %widen.1 = (bf16[4,128,768]{2,1,0:T(8,128)(2,1)}, f32[4,128,768]{2,1,0:T(8,128)}, f32[768,2304]{1,0:T(8,128)}, f32[2,768]{1,0:T(2,128)}, f32[768,768]{1,0:T(8,12...) custom-call(bf16[48,384,384]{2,1,0:T(8,128)(2,1)} %get-tuple-element, ...), custom_call_target="tpu_custom_call" | custom-call | bytes 42467328 | tf_op jit(solution)/shard_map/widen/pallas_call | solution.py:667

commit v6 on v5

--- a/solution.py
+++ b/solution.py
@@ -39,8 +39,8 @@
 PHASES = 2
 OFF = [0, 2, 8, 12, 16, 20, 24, 28, 34, 38]
 OFF_INNER = [0, 2, 8, 13, 17, 21, 25, 29, 35, 39]
-SMALL = [17 + 3 * i for i in range(7)]
-SIDE = ((0, 6, "feed"), (6, 1, "norm"), (7, 6, "attend"), (13, 1, "sums"), (14, 4, "tokens"))
+SMALL = [18 + 4 * i for i in range(7)]
+SIDE = ((0, 6, "feed"), (7, 1, "norm"), (9, 6, "attend"), (15, 1, "sums"), (16, 4, "tokens"))
 VECS = 16
 
 

time: 196 us -> 193 us (0.985)
  Pallas kernels: 195 us -> 192 us
    pallas_call x1, Pallas kernels: 177 us -> 174 us  [run_layer(): pl.pallas_call(layer_kernel, out_shape=[jax.ShapeDtypeStruct((2 * N, BR,...]
where the time goes in v6:
time: 193 us; the launch traced here: 192 us
  Pallas kernels  192 us (99%)
    pallas_call x1, Pallas kernels, run_layer(): pl.pallas_call(layer_kernel, out_shape=[jax.ShapeDtypeStruct((2 * N, BR,...  174 us
    pallas_call x1, Pallas kernels, widen(): pl.pallas_call(widen_kernel, in_specs=[H, V, H, H], out_specs=[H, H, H, V...  17.4 us

profile of v6, /device:TPU:0, one launch (start us, length us, event | category | flops | bytes accessed | tf_op | source)
XLA Modules:
  0.0 192.5 jit_solution(9103644468026319856)
XLA Ops:
  0.7 174.2 %layer.1 = (bf16[48,384,384]{2,1,0:T(8,128)(2,1)}, f32[16,768]{1,0:T(8,128)}, bf16[4,128,768]{2,1,0:T(8,128)(2,1)}, bf16[4,128,768]{2,1,0:T(8,128)(2,1)}) custom-call(s32[4]{0:T(128)} %kinds.1, s32[4]{0:T(128)} %keeps.1, bf16[2,768]{1,0:T(2,128)(2,1)} %proj_bias.1, bf16[768]{0:T(1024)(128)(2,1)} %mix_bias.1, bf16[768]{0:T(1024)(128)(2,1)} %attn_gain.1, ...), custom_call_target="tpu_custom_call" | custom-call | tf_op jit(solution)/shard_map/layer/pallas_call | solution.py:595
  174.9 17.4 %widen.1 = (bf16[4,128,768]{2,1,0:T(8,128)(2,1)}, f32[4,128,768]{2,1,0:T(8,128)}, f32[768,2304]{1,0:T(8,128)}, f32[2,768]{1,0:T(2,128)}, f32[768,768]{1,0:T(8,12...) custom-call(bf16[48,384,384]{2,1,0:T(8,128)(2,1)} %get-tuple-element, ...), custom_call_target="tpu_custom_call" | custom-call | bytes 42467328 | tf_op jit(solution)/shard_map/widen/pallas_call | solution.py:667
